TPU v7x, 512 devices: a whole 4x4x16 slice. The times are simulated.
512 devices in a mesh: along: 32 (over x_lo, z), cross: 16 (over x_hi, y, core).
Axes of the slice: x: 4 (x_hi: 2, x_lo: 2; x = x_hi * 2 + x_lo), y: 4, z: 16, core: 2. Of those that a mesh axis runs over, the one named last changes fastest.
Arguments:
- interface_bins: int32 [2, 7, 512, 2048], P(None, None, 'along', 'cross'), may hold values from 1 to 63
- layer_count: int32 [2, 512, 2048], P(None, 'along', 'cross'), may hold values from 1 to 8
- layer_values: bfloat16 [2, 8, 512, 2048], P(None, None, 'along', 'cross'), may hold values from -6 to 6
- footprint: bfloat16 [33, 33], replicated, may hold values from -0.1875 to 0.1875
- depth_gate: bfloat16 [64, 30], replicated, may hold values from -0.75 to 0.75
Outputs:
- gate_response: float32 [2, 30, 512, 2048], P(None, None, 'along', 'cross')
All inputs are finite; a program needn't handle non-finite values.
Results may differ from a plain program's by a relative error of at most 0.0032.
Values may be sent and summed in bfloat16 or wider, within the bound.
No kernel may reach another device: no remote copies, remote signals or barrier semaphores. Data moves between devices by JAX's collectives and lax.ppermute only.
A program may use at most 128 MiB of HBM per device.

v0:
```python
import functools

import jax
import jax.numpy as jnp
from jax import lax
from jax.experimental import pallas as pl
from jax.experimental.pallas import tpu as pltpu
from jax.sharding import PartitionSpec as P

ROWS = 8
COLS = 16
LANES = 128
BINS = 64
LIMIT = 40 * 1024 * 1024
BF16 = jnp.bfloat16
F32 = jnp.float32

NETWORK = (
    (0, 6), (2, 3), (4, 5),
    (0, 2), (1, 4), (3, 6),
    (0, 1), (2, 5), (3, 4),
    (1, 2), (4, 6),
    (2, 3), (4, 5),
    (1, 2), (3, 4), (5, 6),
)


def lane_group(shape):
    return lax.broadcasted_iota(jnp.int32, shape, len(shape) - 1) // COLS


def swap_groups(parts):
    count = len(parts)
    group = lane_group(parts[0].shape)
    rolled = [pltpu.roll(part, COLS * r, 1) if r else part for r, part in enumerate(parts)]
    current = [rolled[(-m) % count] for m in range(count)]
    step = 1
    while step < count:
        chosen = (group // step) % 2 == 1
        current = [jnp.where(chosen, current[(m - step) % count], current[m]) for m in range(count)]
        step *= 2
    return [
        pltpu.roll(part, (LANES - COLS * k) % LANES, 1) if k else part
        for k, part in enumerate(current)
    ]


def pack_kernel(bounds_ref, count_ref, values_ref, raw_ref, plane_ref):
    samples, layers = values_ref.shape[:2]
    rows = count_ref.shape[1]
    channels = 2 * layers
    for s in range(samples):
        count = count_ref[s]
        keys = [
            jnp.where(k < count - 1, bounds_ref[s, k], BINS).astype(F32) for k in range(layers - 1)
        ]
        for low, high in NETWORK:
            keys[low], keys[high] = (
                jnp.minimum(keys[low], keys[high]),
                jnp.maximum(keys[low], keys[high]),
            )
        planes = keys + [jnp.zeros_like(keys[0])]
        planes += [values_ref[s, k].astype(F32) for k in range(layers)]
        for k, plane in enumerate(planes):
            first = (s * channels + k) * rows
            plane_ref[first : first + rows, :] = plane
    for s in range(samples):
        for q in range(rows // ROWS):
            parts = []
            for r in range(ROWS):
                first = s * channels * rows + q * ROWS + r
                parts.append(plane_ref[pl.ds(first, channels, stride=rows), :])
            for k, block in enumerate(swap_groups(parts)):
                raw_ref[k, q, s * channels : (s + 1) * channels, :] = block.astype(BF16)


def render(raw, store):
    channels = raw.shape[0] // 2
    layers = channels // 2
    level = lax.broadcasted_iota(jnp.int32, (BINS, LANES), 0).astype(F32).astype(BF16)
    wide = raw.astype(F32)
    for s in range(2):

        def row(k):
            line = wide[s * channels + k : s * channels + k + 1, :]
            line = jnp.broadcast_to(line, (16, LANES)).astype(BF16)
            return jnp.concatenate([line] * (BINS // 16), axis=0)

        bins = row(layers)
        for k in range(layers - 1):
            bins = jnp.where(row(k) <= level, row(layers + 1 + k), bins)
        store(s, bins)


def weights(footprint_ref, taps_ref, fan_ref, turned_ref, bands_ref):
    side = footprint_ref.shape[0]
    taps_ref[...] = jnp.zeros_like(taps_ref)
    taps_ref[ROWS : ROWS + side, :side] = footprint_ref[...].astype(F32)
    shape = (LANES, 3 * LANES)
    dy = lax.broadcasted_iota(jnp.int32, shape, 0)
    lane = lax.broadcasted_iota(jnp.int32, shape, 1)
    pick = (dy == COLS * (lane // LANES) - lane % COLS).astype(F32).astype(BF16)
    fan_ref[...] = jnp.dot(taps_ref[...].astype(BF16), pick, preferred_element_type=F32)
    depth = turned_ref.shape[0]
    group = lane_group((depth, LANES))
    for e in range(3):
        lanes = slice(e * LANES, (e + 1) * LANES)
        turned = jnp.zeros((depth, LANES), F32)
        for r in range(ROWS):
            turned = jnp.where(group == r, fan_ref[ROWS - r : ROWS - r + depth, lanes], turned)
        turned_ref[:, lanes] = turned
    shape = (COLS, LANES)
    later = lax.broadcasted_iota(jnp.int32, shape, 1) % COLS >= lax.broadcasted_iota(
        jnp.int32, shape, 0
    )
    nothing = jnp.zeros((LANES, LANES), BF16)
    for dq in range(depth // ROWS):
        bands_ref[dq, 0, :, LANES:] = nothing
        bands_ref[dq, 3, :, :LANES] = nothing
        for r in range(ROWS):
            at = dq * ROWS + r
            lines = [
                jnp.broadcast_to(turned_ref[at : at + 1, e * LANES : (e + 1) * LANES], shape)
                for e in range(3)
            ]
            same = [pltpu.roll(line, 0, 1, stride=1, stride_axis=0) for line in lines]
            next_ = [
                pltpu.roll(line, LANES - COLS, 1, stride=1, stride_axis=0) for line in lines[1:]
            ]
            next_.append(jnp.zeros(shape, F32))
            for e in range(3):
                block = jnp.where(later, same[e], next_[e]).astype(BF16)
                span = slice(r * COLS, (r + 1) * COLS)
                bands_ref[dq, e, span, :LANES] = block
                bands_ref[dq, e + 1, span, LANES:] = block


def own_kernel(
    raw_ref, footprint_ref, gates_ref, own_ref, bands_ref, mix_ref, taps_ref, fan_ref, turned_ref, mixed_ref
):
    weights(footprint_ref, taps_ref, fan_ref, turned_ref, bands_ref)
    gates, bins = gates_ref.shape
    half = mix_ref.shape[0] // 2
    mixed_ref[...] = jnp.zeros_like(mixed_ref)
    for s in range(2):
        mixed_ref[s * half : s * half + gates, s * bins : (s + 1) * bins] = gates_ref[...].astype(F32)
    mix_ref[...] = mixed_ref[...].astype(BF16)
    blocks, groups = raw_ref.shape[:2]

    @pl.loop(0, blocks)
    def _(k):
        for q in range(groups):

            def store(s, block):
                own_ref[k, q, s * BINS : (s + 1) * BINS, :] = block

            render(raw_ref[k, q], store)


def edge_kernel(before_ref, raw_ref, after_ref, last_ref, first_ref):
    groups = raw_ref.shape[1]
    for target, k in ((last_ref, raw_ref.shape[0] - 1), (first_ref, 0)):
        for at, source in enumerate((before_ref, raw_ref, after_ref)):
            target[at * groups : (at + 1) * groups] = source[k]


def middle_kernel(
    before_ref, own_ref, after_ref, bands_ref, mix_ref, part_ref, mid_ref, around_ref
):
    blocks, groups = before_ref.shape[:2]
    for at, source in enumerate((before_ref, after_ref)):

        @pl.loop(0, blocks)
        def _(k):
            for q in range(groups):

                def store(s, block):
                    around_ref[at, k, q, s * BINS : (s + 1) * BINS, :] = block

                render(source[k, q], store)

    def piece(k, q):
        if q < groups:
            return around_ref[0, k, q]
        if q < 2 * groups:
            return own_ref[k, q - groups]
        return around_ref[1, k, q - 2 * groups]

    reach = bands_ref.shape[0]
    pairs = blocks // 2
    for pair in range(pairs):
        inner = [j for j in range(4) if 0 <= 2 * pair + j - 1 < blocks]
        total = None
        for dq in range(reach):
            left = jnp.concatenate(
                [
                    jnp.concatenate([piece(2 * pair + j - 1, a + dq) for j in inner], axis=1)
                    for a in range(groups)
                ],
                axis=0,
            )
            right = bands_ref[dq, inner[0] : inner[-1] + 1].reshape(len(inner) * LANES, 2 * LANES)
            term = jnp.dot(left, right, preferred_element_type=F32)
            total = term if total is None else total + term
        depth = total.shape[0] // groups
        for side in range(2):
            block = 2 * pair + side
            lanes = slice(side * LANES, (side + 1) * LANES)
            if block == 0:
                part_ref[0] = total[:, lanes]
            elif block == blocks - 1:
                part_ref[1] = total[:, lanes]
            else:
                for a in range(groups):
                    smooth = total[a * depth : (a + 1) * depth, lanes].astype(BF16)
                    mid_ref[a, block - 1] = jnp.dot(
                        mix_ref[...], smooth, preferred_element_type=F32
                    )


def finish_kernel(left_ref, right_ref, bands_ref, mix_ref, part_ref, mid_ref, out_ref, halo_ref):
    spans = left_ref.shape[0]
    groups, mids = mid_ref.shape[:2]
    reach = bands_ref.shape[0]

    @pl.loop(0, spans)
    def _(q):
        for at, source in enumerate((left_ref, right_ref)):

            def store(s, block):
                halo_ref[at, q, s * BINS : (s + 1) * BINS, :] = block

            render(source[q], store)

    ends = []
    for at, (j, lanes) in enumerate(((0, slice(0, LANES)), (3, slice(LANES, 2 * LANES)))):
        left = jnp.concatenate(
            [
                jnp.concatenate([halo_ref[at, a + dq] for dq in range(reach)], axis=1)
                for a in range(groups)
            ],
            axis=0,
        )
        right = jnp.concatenate([bands_ref[dq, j, :, lanes] for dq in range(reach)], axis=0)
        total = part_ref[at] + jnp.dot(left, right, preferred_element_type=F32)
        depth = total.shape[0] // groups
        ends.append(
            [
                jnp.dot(
                    mix_ref[...],
                    total[a * depth : (a + 1) * depth].astype(BF16),
                    preferred_element_type=F32,
                )
                for a in range(groups)
            ]
        )
    half = mix_ref.shape[0] // 2
    rows = groups * ROWS
    gates = out_ref.shape[0] // (2 * rows)
    for a in range(groups):
        for s in range(2):
            span = slice(s * half, (s + 1) * half)
            parts = [ends[0][a][span]]
            parts += [mid_ref[a, k, span, :] for k in range(mids)]
            parts += [ends[1][a][span]]
            for r, block in enumerate(swap_groups(parts)):
                first = s * gates * rows + a * ROWS + r
                out_ref[pl.ds(first, gates, stride=rows), :] = block[:gates]


def vmem(*shape, dtype=BF16):
    return pltpu.VMEM(shape, dtype)


def near(*arrays):
    return [pltpu.with_memory_space_constraint(array, pltpu.VMEM) for array in arrays]


def call(kernel, out, scratch, args, flops=0, moved=0):
    whole = pl.BlockSpec(memory_space=pltpu.VMEM)
    many = isinstance(out, (list, tuple))
    return pl.pallas_call(
        kernel,
        out_shape=out,
        in_specs=[whole] * len(args),
        out_specs=[whole] * len(out) if many else whole,
        scratch_shapes=scratch,
        compiler_params=pltpu.CompilerParams(vmem_limit_bytes=LIMIT),
        cost_estimate=pl.CostEstimate(flops=flops, bytes_accessed=moved, transcendentals=0),
    )(*args)


def shifted(array, axis, ahead):
    count = lax.axis_size(axis)
    pairs = [(i, i + 1) if ahead else (i + 1, i) for i in range(count - 1)]
    return lax.ppermute(array, axis, pairs)


def local(interface_bins, layer_count, layer_values, footprint, depth_gate):
    samples, layers, rows, width = layer_values.shape
    gates = depth_gate.shape[1]
    blocks, groups, channels = width // COLS, rows // ROWS, 2 * layers * samples
    reach = (footprint.shape[0] + ROWS - 1) // ROWS
    deep = samples * BINS

    raw = call(
        pack_kernel,
        vmem(blocks, groups, channels, LANES),
        [vmem(channels * rows, width, dtype=F32)],
        (interface_bins, layer_count, layer_values),
    )
    before = shifted(raw, "along", True)
    after = shifted(raw, "along", False)
    own, bands, mix = call(
        own_kernel,
        [
            vmem(blocks, groups, deep, LANES),
            vmem(reach, 4, LANES, 2 * LANES),
            vmem(64, deep),
        ],
        [
            vmem(64, LANES, dtype=F32),
            vmem(64, 3 * LANES, dtype=F32),
            vmem(reach * ROWS, 3 * LANES, dtype=F32),
            vmem(64, deep, dtype=F32),
        ],
        (*near(raw), footprint, depth_gate.T),
        flops=2_000_000_000,
        moved=4_000_000,
    )
    last, first = call(
        edge_kernel,
        [vmem(3 * groups, channels, LANES)] * 2,
        [],
        near(before, raw, after),
    )
    left = shifted(last, "cross", True)
    right = shifted(first, "cross", False)
    part, mid = call(
        middle_kernel,
        [
            vmem(2, groups * deep, LANES, dtype=F32),
            vmem(groups, blocks - 2, 64, LANES, dtype=F32),
        ],
        [vmem(2, blocks, groups, deep, LANES)],
        near(before, own, after, bands, mix),
        flops=3_000_000_000,
        moved=4_000_000,
    )
    out = call(
        finish_kernel,
        jax.ShapeDtypeStruct((samples * gates * rows, width), F32),
        [vmem(2, 3 * groups, deep, LANES)],
        near(left, right, bands, mix, part, mid),
    )
    return out.reshape(samples, gates, rows, width)


def solution(mesh):
    in_specs = (
        P(None, None, "along", "cross"),
        P(None, "along", "cross"),
        P(None, None, "along", "cross"),
        P(),
        P(),
    )
    out_specs = P(None, None, "along", "cross")
    return jax.shard_map(local, mesh=mesh, in_specs=in_specs, out_specs=out_specs, check_vma=False)
```

profile of v0, /device:TPU:6, one launch (start us, length us, event | category | flops | bytes accessed | tf_op | source)
XLA Modules:
  0.0 39.0 jit_solution(5596298809648785430)
XLA Ops:
  0.0 0.0 copy-start
  0.0 0.9 %copy-done = s32[2,7,16,128]{3,2,1,0:T(8,128)S(1)} copy-done((s32[2,7,16,128]{3,2,1,0:T(8,128)S(1)}, s32[2,7,16,128]{3,2,1,0:T(8,128)}, u32[]{:S(2)}) %copy-start) | copy-done | bytes 114712
  0.9 0.0 copy-start.1
  0.9 0.8 %copy-done.1 = bf16[2,8,16,128]{3,2,1,0:T(8,128)(2,1)S(1)} copy-done((bf16[2,8,16,128]{3,2,1,0:T(8,128)(2,1)S(1)}, bf16[2,8,16,128]{3,2,1,0:T(8,128)(2,1)}, u32[]{:S(2)}) %copy-start.1) | copy-done | bytes 65560
  1.7 0.0 copy-start.2
  1.7 0.7 %copy-done.2 = s32[2,16,128]{2,1,0:T(8,128)S(1)} copy-done((s32[2,16,128]{2,1,0:T(8,128)S(1)}, s32[2,16,128]{2,1,0:T(8,128)}, u32[]{:S(2)}) %copy-start.2) | copy-done | bytes 16408
  2.5 0.3 shard_map.55.raw_ref
  2.7 11.7 %collective-permute-start.1 = (bf16[8,2,32,128]{3,2,1,0:T(8,128)(2,1)S(1)}, bf16[8,2,32,128]{3,2,1,0:T(8,128)(2,1)S(1)}, u32[]{:S(2)}, u32[]{:S(2)}) collective-permute-start(bf16[8,2,32,128]{3,2,1,0:T(8,128)(2,1)S(1)} %shard_map.55.raw_ref), channel_id=1, source_target_pairs={{16,0},{32,16},{48,32},{64,48},{80,64},{96,80},{112,96},{128,112},... | collective-permute-start | bytes 393224 | tf_op jit(solution)/shard_map/ppermute | solution.py:296
  14.4 1.9 %collective-permute-start = (bf16[8,2,32,128]{3,2,1,0:T(8,128)(2,1)S(1)}, bf16[8,2,32,128]{3,2,1,0:T(8,128)(2,1)S(1)}, u32[]{:S(2)}, u32[]{:S(2)}) collective-permute-start(bf16[8,2,32,128]{3,2,1,0:T(8,128)(2,1)S(1)} %shard_map.55.raw_ref), channel_id=1, source_target_pairs={{0,16},{16,32},{32,48},{48,64},{64,80},{80,96},{96,112},{112,128},... | collective-permute-start | bytes 393224 | tf_op jit(solution)/shard_map/ppermute | solution.py:296
  16.3 0.0 copy-start.3
  16.4 0.7 %copy-done.3 = bf16[33,33]{1,0:T(8,128)(2,1)S(1)} copy-done((bf16[33,33]{1,0:T(8,128)(2,1)S(1)}, bf16[33,33]{1,0:T(8,128)(2,1)}, u32[]{:S(2)}) %copy-start.3) | copy-done | bytes 2202
  17.1 0.0 copy-start.4
  17.1 0.7 %copy-done.4 = bf16[64,30]{0,1:T(8,128)(2,1)S(1)} copy-done((bf16[64,30]{0,1:T(8,128)(2,1)S(1)}, bf16[64,30]{0,1:T(8,128)(2,1)}, u32[]{:S(2)}) %copy-start.4) | copy-done | bytes 3864
  17.7 1.0 %shard_map.57 = (bf16[8,2,128,128]{3,2,1,0:T(8,128)(2,1)S(1)}, bf16[5,4,128,256]{3,2,1,0:T(8,128)(2,1)S(1)}, bf16[64,128]{1,0:T(8,128)(2,1)S(1)}) custom-call(bf16[8,2,32,128]{3,2,1,0:T(8,128)(2,1)S(1)} %shard_map.55.raw_ref, bf16[33,33]{1,0:T(8,128)(2,1)S(1)} %copy-done.3, bf16[30,64]{1,0:T(8,128)(2,1)S(1)} %bitcast.2), custom_call_target="tpu_custom_call" | custom-call | flops 2000000000 | bytes 4000000 | tf_op jit(solution)/shard_map/pallas_call | solution.py:282
  18.7 0.0 collective-permute-done.1.after_ref
  18.7 4.7 %collective-permute-done.before_ref = bf16[8,2,32,128]{3,2,1,0:T(8,128)(2,1)S(1)} collective-permute-done((bf16[8,2,32,128]{3,2,1,0:T(8,128)(2,1)S(1)}, bf16[8,2,32,128]{3,2,1,0:T(8,128)(2,1)S(1)}, u32[]{:S(2)}, u32[]{:S(2)}) %collective-permute-start) | collective-permute-done | bytes 131104 | tf_op jit(solution)/shard_map/ppermute | solution.py:296
  23.5 1.9 %collective-permute-start.2 = (bf16[6,32,128]{2,1,0:T(8,128)(2,1)S(1)}, bf16[6,32,128]{2,1,0:T(8,128)(2,1)S(1)}, u32[]{:S(2)}, u32[]{:S(2)}) collective-permute-start(bf16[6,32,128]{2,1,0:T(8,128)(2,1)S(1)} %get-tuple-element.12), channel_id=1, source_target_pairs={{0,1},{1,2},{2,3},{3,4},{4,5},{5,6},{6,7},{7,8},{8,9},{9,10},{10,1... | collective-permute-start | bytes 147464 | tf_op jit(solution)/shard_map/ppermute | solution.py:296
  25.4 7.3 %collective-permute-start.3 = (bf16[6,32,128]{2,1,0:T(8,128)(2,1)S(1)}, bf16[6,32,128]{2,1,0:T(8,128)(2,1)S(1)}, u32[]{:S(2)}, u32[]{:S(2)}) collective-permute-start(bf16[6,32,128]{2,1,0:T(8,128)(2,1)S(1)} %get-tuple-element.13), channel_id=1, source_target_pairs={{1,0},{2,1},{3,2},{4,3},{5,4},{6,5},{7,6},{8,7},{9,8},{10,9},{11,1... | collective-permute-start | bytes 147464 | tf_op jit(solution)/shard_map/ppermute | solution.py:296
  32.7 4.3 %shard_map.58 = (f32[2,256,128]{2,1,0:T(8,128)S(1)}, f32[2,6,64,128]{3,2,1,0:T(8,128)S(1)}) custom-call(bf16[8,2,32,128]{3,2,1,0:T(8,128)(2,1)S(1)} %collective-permute-done.before_ref, bf16[8,2,128,128]{3,2,1,0:T(8,128)(2,1)S(1)} %get-tuple-element.16.own_ref, bf16[8,2,32,128]{3,2,1,0:T(8,128)(2,1)S(1)} %collective-permute-done.1.after_ref, ...), custom_call_target="tpu_custom_call" | custom-call | flops 3000000000 | bytes 4000000 | tf_op jit(solution)/shard_map/pallas_call | solution.py:282
  37.0 0.0 collective-permute-done.2.left_ref
  37.0 0.0 collective-permute-done.3.right_ref
  37.0 1.9 %shard_map.59 = f32[960,128]{1,0:T(8,128)} custom-call(bf16[6,32,128]{2,1,0:T(8,128)(2,1)S(1)} %collective-permute-done.2.left_ref, bf16[6,32,128]{2,1,0:T(8,128)(2,1)S(1)} %collective-permute-done.3.right_ref, bf16[5,4,128,256]{3,2,1,0:T(8,128)(2,1)S(1)} %get-tuple-element.14.bands_ref, bf16[64,128]{1,0:T(8,128)(2,1)S(1)} %get-tuple-element.15.mix_ref, ...), custom_call_target="tpu_custom_call" | custom-call | tf_op jit(solution)/shard_map/pallas_call | solution.py:282
  (1 shorter events, 0.0 us)
Async XLA Ops:
  0.0 0.9 %copy-start = (s32[2,7,16,128]{3,2,1,0:T(8,128)S(1)}, s32[2,7,16,128]{3,2,1,0:T(8,128)}, u32[]{:S(2)}) copy-start(s32[2,7,16,128]{3,2,1,0:T(8,128)} %bounds_ref.1) | copy-start | bytes 344068
  0.9 0.8 %copy-start.1 = (bf16[2,8,16,128]{3,2,1,0:T(8,128)(2,1)S(1)}, bf16[2,8,16,128]{3,2,1,0:T(8,128)(2,1)}, u32[]{:S(2)}) copy-start(bf16[2,8,16,128]{3,2,1,0:T(8,128)(2,1)} %values_ref.1) | copy-start | bytes 196612
  1.7 0.7 %copy-start.2 = (s32[2,16,128]{2,1,0:T(8,128)S(1)}, s32[2,16,128]{2,1,0:T(8,128)}, u32[]{:S(2)}) copy-start(s32[2,16,128]{2,1,0:T(8,128)} %count_ref.1) | copy-start | bytes 49156
  2.7 16.0 %collective-permute-start.1 = (bf16[8,2,32,128]{3,2,1,0:T(8,128)(2,1)S(1)}, bf16[8,2,32,128]{3,2,1,0:T(8,128)(2,1)S(1)}, u32[]{:S(2)}, u32[]{:S(2)}) collective-permute-start(bf16[8,2,32,128]{3,2,1,0:T(8,128)(2,1)S(1)} %shard_map.55.raw_ref), channel_id=1, source_target_pairs={{16,0},{32,16},{48,32},{64,48},{80,64},{96,80},{112,96},{128,112},... | collective-permute-start | bytes 393224 | tf_op jit(solution)/shard_map/ppermute | solution.py:296
  14.4 9.0 %collective-permute-start = (bf16[8,2,32,128]{3,2,1,0:T(8,128)(2,1)S(1)}, bf16[8,2,32,128]{3,2,1,0:T(8,128)(2,1)S(1)}, u32[]{:S(2)}, u32[]{:S(2)}) collective-permute-start(bf16[8,2,32,128]{3,2,1,0:T(8,128)(2,1)S(1)} %shard_map.55.raw_ref), channel_id=1, source_target_pairs={{0,16},{16,32},{32,48},{48,64},{64,80},{80,96},{96,112},{112,128},... | collective-permute-start | bytes 393224 | tf_op jit(solution)/shard_map/ppermute | solution.py:296
  16.3 0.7 %copy-start.3 = (bf16[33,33]{1,0:T(8,128)(2,1)S(1)}, bf16[33,33]{1,0:T(8,128)(2,1)}, u32[]{:S(2)}) copy-start(bf16[33,33]{1,0:T(8,128)(2,1)} %footprint_ref.1) | copy-start | bytes 6538
  17.1 0.7 %copy-start.4 = (bf16[64,30]{0,1:T(8,128)(2,1)S(1)}, bf16[64,30]{0,1:T(8,128)(2,1)}, u32[]{:S(2)}) copy-start(bf16[64,30]{0,1:T(8,128)(2,1)} %param.9) | copy-start | bytes 11524
  23.5 13.5 %collective-permute-start.2 = (bf16[6,32,128]{2,1,0:T(8,128)(2,1)S(1)}, bf16[6,32,128]{2,1,0:T(8,128)(2,1)S(1)}, u32[]{:S(2)}, u32[]{:S(2)}) collective-permute-start(bf16[6,32,128]{2,1,0:T(8,128)(2,1)S(1)} %get-tuple-element.12), channel_id=1, source_target_pairs={{0,1},{1,2},{2,3},{3,4},{4,5},{5,6},{6,7},{7,8},{8,9},{9,10},{10,1... | collective-permute-start | bytes 147464 | tf_op jit(solution)/shard_map/ppermute | solution.py:296
  25.4 11.6 %collective-permute-start.3 = (bf16[6,32,128]{2,1,0:T(8,128)(2,1)S(1)}, bf16[6,32,128]{2,1,0:T(8,128)(2,1)S(1)}, u32[]{:S(2)}, u32[]{:S(2)}) collective-permute-start(bf16[6,32,128]{2,1,0:T(8,128)(2,1)S(1)} %get-tuple-element.13), channel_id=1, source_target_pairs={{1,0},{2,1},{3,2},{4,3},{5,4},{6,5},{7,6},{8,7},{9,8},{10,9},{11,1... | collective-permute-start | bytes 147464 | tf_op jit(solution)/shard_map/ppermute | solution.py:296
where the time goes:
time: 39.4 us; the launch traced here: 39 us
  starting transfers between devices  22.8 us (58%)
  Pallas kernels  7.56 us (19%)
  waiting for transfers between devices  4.72 us (12%)
  local copies, waits for them, and re-layouts  3.85 us (10%)
    ppermute x4, starting transfers between devices, shifted(): return lax.ppermute(array, axis, pairs)  22.8 us
    pallas_call x5, Pallas kernels, call(): pl.pallas_call(kernel, out_shape=out, in_specs=[whole] * len(args), out_s...  7.56 us
    ppermute x4, waiting for transfers between devices, shifted(): return lax.ppermute(array, axis, pairs)  4.72 us
    unnamed x10, local copies, waits for them, and re-layouts  3.85 us
  transfers between devices with their start and end apart: 4, of which 1 were waited for; matrix products, arithmetic and copies ran while one was open for 0% of the time, Pallas kernels for 14%

commit v1 on v0

--- a/solution.py
+++ b/solution.py
@@ -45,7 +45,23 @@
     ]
 
 
-def pack_kernel(bounds_ref, count_ref, values_ref, raw_ref, plane_ref):
+def fetch(sources, targets, sems):
+    copies = [
+        pltpu.make_async_copy(source, target, sems.at[at])
+        for at, (source, target) in enumerate(zip(sources, targets))
+    ]
+    for copy in copies:
+        copy.start()
+    return copies
+
+
+def pack_kernel(
+    bounds_hbm, count_hbm, values_hbm, raw_ref, plane_ref, bounds_ref, count_ref, values_ref, sems
+):
+    for copy in fetch(
+        (bounds_hbm, count_hbm, values_hbm), (bounds_ref, count_ref, values_ref), sems
+    ):
+        copy.wait()
     samples, layers = values_ref.shape[:2]
     rows = count_ref.shape[1]
     channels = 2 * layers
@@ -136,8 +152,34 @@
 
 
 def own_kernel(
-    raw_ref, footprint_ref, gates_ref, own_ref, bands_ref, mix_ref, taps_ref, fan_ref, turned_ref, mixed_ref
+    raw_ref,
+    footprint_hbm,
+    gates_hbm,
+    own_ref,
+    bands_ref,
+    mix_ref,
+    taps_ref,
+    fan_ref,
+    turned_ref,
+    mixed_ref,
+    footprint_ref,
+    gates_ref,
+    sems,
 ):
+    copies = fetch((footprint_hbm, gates_hbm), (footprint_ref, gates_ref), sems)
+    blocks, groups = raw_ref.shape[:2]
+
+    @pl.loop(0, blocks)
+    def _(k):
+        for q in range(groups):
+
+            def store(s, block):
+                own_ref[k, q, s * BINS : (s + 1) * BINS, :] = block
+
+            render(raw_ref[k, q], store)
+
+    for copy in copies:
+        copy.wait()
     weights(footprint_ref, taps_ref, fan_ref, turned_ref, bands_ref)
     gates, bins = gates_ref.shape
     half = mix_ref.shape[0] // 2
@@ -145,27 +187,22 @@
     for s in range(2):
         mixed_ref[s * half : s * half + gates, s * bins : (s + 1) * bins] = gates_ref[...].astype(F32)
     mix_ref[...] = mixed_ref[...].astype(BF16)
-    blocks, groups = raw_ref.shape[:2]
-
-    @pl.loop(0, blocks)
-    def _(k):
-        for q in range(groups):
-
-            def store(s, block):
-                own_ref[k, q, s * BINS : (s + 1) * BINS, :] = block
-
-            render(raw_ref[k, q], store)
-
-
-def edge_kernel(before_ref, raw_ref, after_ref, last_ref, first_ref):
+
+
+def parity():
+    return lax.rem(lax.axis_index("cross"), 2)
+
+
+def edge_kernel(after_ref, raw_ref, before_ref, outer_ref, inner_ref):
     groups = raw_ref.shape[1]
-    for target, k in ((last_ref, raw_ref.shape[0] - 1), (first_ref, 0)):
+    end = raw_ref.shape[0] - 1
+    for target, k in ((outer_ref, end * parity()), (inner_ref, end * (1 - parity()))):
         for at, source in enumerate((before_ref, raw_ref, after_ref)):
             target[at * groups : (at + 1) * groups] = source[k]
 
 
 def middle_kernel(
-    before_ref, own_ref, after_ref, bands_ref, mix_ref, part_ref, mid_ref, around_ref
+    after_ref, own_ref, before_ref, bands_ref, mix_ref, part_ref, mid_ref, around_ref
 ):
     blocks, groups = before_ref.shape[:2]
     for at, source in enumerate((before_ref, after_ref)):
@@ -218,14 +255,14 @@
                     )
 
 
-def finish_kernel(left_ref, right_ref, bands_ref, mix_ref, part_ref, mid_ref, out_ref, halo_ref):
-    spans = left_ref.shape[0]
+def finish_kernel(outer_ref, inner_ref, bands_ref, mix_ref, part_ref, mid_ref, out_ref, halo_ref):
+    spans = outer_ref.shape[0]
     groups, mids = mid_ref.shape[:2]
     reach = bands_ref.shape[0]
 
     @pl.loop(0, spans)
     def _(q):
-        for at, source in enumerate((left_ref, right_ref)):
+        for at, source in ((parity(), outer_ref), (1 - parity(), inner_ref)):
 
             def store(s, block):
                 halo_ref[at, q, s * BINS : (s + 1) * BINS, :] = block
@@ -272,28 +309,41 @@
     return pltpu.VMEM(shape, dtype)
 
 
+def far(*arrays):
+    return [pltpu.with_memory_space_constraint(array, pltpu.HBM) for array in arrays]
+
+
 def near(*arrays):
     return [pltpu.with_memory_space_constraint(array, pltpu.VMEM) for array in arrays]
 
 
-def call(kernel, out, scratch, args, flops=0, moved=0):
+def call(kernel, out, scratch, args, remote=(), flops=0, moved=0):
     whole = pl.BlockSpec(memory_space=pltpu.VMEM)
     many = isinstance(out, (list, tuple))
+    if remote:
+        scratch = scratch + [pltpu.VMEM(array.shape, array.dtype) for array in remote]
+        scratch.append(pltpu.SemaphoreType.DMA((len(remote),)))
     return pl.pallas_call(
         kernel,
         out_shape=out,
-        in_specs=[whole] * len(args),
+        in_specs=[whole] * len(args) + [pl.BlockSpec(memory_space=pl.ANY)] * len(remote),
         out_specs=[whole] * len(out) if many else whole,
         scratch_shapes=scratch,
         compiler_params=pltpu.CompilerParams(vmem_limit_bytes=LIMIT),
         cost_estimate=pl.CostEstimate(flops=flops, bytes_accessed=moved, transcendentals=0),
-    )(*args)
+    )(*near(*args), *far(*remote))
 
 
 def shifted(array, axis, ahead):
     count = lax.axis_size(axis)
     pairs = [(i, i + 1) if ahead else (i + 1, i) for i in range(count - 1)]
     return lax.ppermute(array, axis, pairs)
+
+
+def exchanged(array, axis, first):
+    count = lax.axis_size(axis)
+    pairs = [(i, i + 1) for i in range(first, count - 1, 2)]
+    return lax.ppermute(array, axis, pairs + [(j, i) for i, j in pairs])
 
 
 def local(interface_bins, layer_count, layer_values, footprint, depth_gate):
@@ -307,10 +357,11 @@
         pack_kernel,
         vmem(blocks, groups, channels, LANES),
         [vmem(channels * rows, width, dtype=F32)],
-        (interface_bins, layer_count, layer_values),
-    )
+        (),
+        remote=(interface_bins, layer_count, layer_values),
+    )
+    after = shifted(raw, "along", False)
     before = shifted(raw, "along", True)
-    after = shifted(raw, "along", False)
     own, bands, mix = call(
         own_kernel,
         [
@@ -324,18 +375,19 @@
             vmem(reach * ROWS, 3 * LANES, dtype=F32),
             vmem(64, deep, dtype=F32),
         ],
-        (*near(raw), footprint, depth_gate.T),
+        (raw,),
+        remote=(footprint, depth_gate.T),
         flops=2_000_000_000,
         moved=4_000_000,
     )
-    last, first = call(
+    outer, inner = call(
         edge_kernel,
         [vmem(3 * groups, channels, LANES)] * 2,
         [],
-        near(before, raw, after),
-    )
-    left = shifted(last, "cross", True)
-    right = shifted(first, "cross", False)
+        (after, raw, before),
+    )
+    outer = exchanged(outer, "cross", 1)
+    inner = exchanged(inner, "cross", 0)
     part, mid = call(
         middle_kernel,
         [
@@ -343,7 +395,7 @@
             vmem(groups, blocks - 2, 64, LANES, dtype=F32),
         ],
         [vmem(2, blocks, groups, deep, LANES)],
-        near(before, own, after, bands, mix),
+        (after, own, before, bands, mix),
         flops=3_000_000_000,
         moved=4_000_000,
     )
@@ -351,7 +403,7 @@
         finish_kernel,
         jax.ShapeDtypeStruct((samples * gates * rows, width), F32),
         [vmem(2, 3 * groups, deep, LANES)],
-        near(left, right, bands, mix, part, mid),
+        (outer, inner, bands, mix, part, mid),
     )
     return out.reshape(samples, gates, rows, width)
 

time: 39.4 us -> 30.9 us (0.78)
  the two profiles are of different devices: /device:TPU:6 before, /device:TPU:7 now
where the time goes in v1:
time: 30.9 us; the launch traced here: 30.5 us
  starting transfers between devices  20.8 us (67%)
  Pallas kernels  8.8 us (28%)
  waiting for transfers between devices  0.87 us (3%)
    ppermute x2, starting transfers between devices, shifted(): return lax.ppermute(array, axis, pairs)  13.3 us
    pallas_call x5, Pallas kernels, call(): pl.pallas_call(kernel, out_shape=out, in_specs=[whole] * len(args) + [pl....  8.8 us
    ppermute x2, starting transfers between devices, exchanged(): return lax.ppermute(array, axis, pairs + [(j, i) for i, j in pairs])  7.48 us
    ppermute x2, waiting for transfers between devices, shifted(): return lax.ppermute(array, axis, pairs)  0.86 us
  transfers between devices with their start and end apart: 4, of which 1 were waited for; matrix products, arithmetic and copies ran while one was open for 0% of the time, Pallas kernels for 18%

profile of v1, /device:TPU:7, one launch (start us, length us, event | category | flops | bytes accessed | tf_op | source)
XLA Modules:
  0.0 30.5 jit_solution(2642171103511412161)
XLA Ops:
  0.0 1.2 %shard_map.55.raw_ref = bf16[8,2,32,128]{3,2,1,0:T(8,128)(2,1)S(1)} custom-call(s32[2,7,16,128]{3,2,1,0:T(8,128)} %bounds_hbm.1, s32[2,16,128]{2,1,0:T(8,128)} %count_hbm.1, bf16[2,8,16,128]{3,2,1,0:T(8,128)(2,1)} %values_hbm.1), custom_call_target="tpu_custom_call" | custom-call | tf_op jit(solution)/shard_map/pallas_call | solution.py:326
  1.2 3.5 %collective-permute-start.1 = (bf16[8,2,32,128]{3,2,1,0:T(8,128)(2,1)S(1)}, bf16[8,2,32,128]{3,2,1,0:T(8,128)(2,1)S(1)}, u32[]{:S(2)}, u32[]{:S(2)}) collective-permute-start(bf16[8,2,32,128]{3,2,1,0:T(8,128)(2,1)S(1)} %shard_map.55.raw_ref), channel_id=1, source_target_pairs={{0,16},{16,32},{32,48},{48,64},{64,80},{80,96},{96,112},{112,128},... | collective-permute-start | bytes 393224 | tf_op jit(solution)/shard_map/ppermute | solution.py:340
  4.8 9.8 %collective-permute-start = (bf16[8,2,32,128]{3,2,1,0:T(8,128)(2,1)S(1)}, bf16[8,2,32,128]{3,2,1,0:T(8,128)(2,1)S(1)}, u32[]{:S(2)}, u32[]{:S(2)}) collective-permute-start(bf16[8,2,32,128]{3,2,1,0:T(8,128)(2,1)S(1)} %shard_map.55.raw_ref), channel_id=1, source_target_pairs={{16,0},{32,16},{48,32},{64,48},{80,64},{96,80},{112,96},{128,112},... | collective-permute-start | bytes 393224 | tf_op jit(solution)/shard_map/ppermute | solution.py:340
  14.6 1.3 %shard_map.57 = (bf16[8,2,128,128]{3,2,1,0:T(8,128)(2,1)S(1)}, bf16[5,4,128,256]{3,2,1,0:T(8,128)(2,1)S(1)}, bf16[64,128]{1,0:T(8,128)(2,1)S(1)}) custom-call(bf16[8,2,32,128]{3,2,1,0:T(8,128)(2,1)S(1)} %shard_map.55.raw_ref, bf16[33,33]{1,0:T(8,128)(2,1)} %footprint_hbm.1, bf16[30,64]{1,0:T(8,128)(2,1)} %bitcast.2), custom_call_target="tpu_custom_call" | custom-call | flops 2000000000 | bytes 4000000 | tf_op jit(solution)/shard_map/pallas_call | solution.py:326
  15.8 0.0 collective-permute-done.1.before_ref
  15.8 0.9 %collective-permute-done.after_ref = bf16[8,2,32,128]{3,2,1,0:T(8,128)(2,1)S(1)} collective-permute-done((bf16[8,2,32,128]{3,2,1,0:T(8,128)(2,1)S(1)}, bf16[8,2,32,128]{3,2,1,0:T(8,128)(2,1)S(1)}, u32[]{:S(2)}, u32[]{:S(2)}) %collective-permute-start) | collective-permute-done | bytes 131104 | tf_op jit(solution)/shard_map/ppermute | solution.py:340
  16.7 4.6 %collective-permute-start.2 = (bf16[6,32,128]{2,1,0:T(8,128)(2,1)S(1)}, bf16[6,32,128]{2,1,0:T(8,128)(2,1)S(1)}, u32[]{:S(2)}, u32[]{:S(2)}) collective-permute-start(bf16[6,32,128]{2,1,0:T(8,128)(2,1)S(1)} %get-tuple-element.12), channel_id=1, source_target_pairs={{1,2},{3,4},{5,6},{7,8},{9,10},{11,12},{13,14},{2,1},{4,3},{6,5},{... | collective-permute-start | bytes 147464 | tf_op jit(solution)/shard_map/ppermute | solution.py:346
  21.3 2.9 %collective-permute-start.3 = (bf16[6,32,128]{2,1,0:T(8,128)(2,1)S(1)}, bf16[6,32,128]{2,1,0:T(8,128)(2,1)S(1)}, u32[]{:S(2)}, u32[]{:S(2)}) collective-permute-start(bf16[6,32,128]{2,1,0:T(8,128)(2,1)S(1)} %get-tuple-element.13), channel_id=1, source_target_pairs={{0,1},{2,3},{4,5},{6,7},{8,9},{10,11},{12,13},{14,15},{1,0},{3,2},... | collective-permute-start | bytes 147464 | tf_op jit(solution)/shard_map/ppermute | solution.py:346
  24.2 4.3 %shard_map.58 = (f32[2,256,128]{2,1,0:T(8,128)S(1)}, f32[2,6,64,128]{3,2,1,0:T(8,128)S(1)}) custom-call(bf16[8,2,32,128]{3,2,1,0:T(8,128)(2,1)S(1)} %collective-permute-done.after_ref, bf16[8,2,128,128]{3,2,1,0:T(8,128)(2,1)S(1)} %get-tuple-element.16.own_ref, bf16[8,2,32,128]{3,2,1,0:T(8,128)(2,1)S(1)} %collective-permute-done.1.before_ref, ...), custom_call_target="tpu_custom_call" | custom-call | flops 3000000000 | bytes 4000000 | tf_op jit(solution)/shard_map/pallas_call | solution.py:326
  28.5 0.0 collective-permute-done.2.outer_ref
  28.6 0.0 collective-permute-done.3.inner_ref
  28.6 2.0 %shard_map.59 = f32[960,128]{1,0:T(8,128)} custom-call(bf16[6,32,128]{2,1,0:T(8,128)(2,1)S(1)} %collective-permute-done.2.outer_ref, bf16[6,32,128]{2,1,0:T(8,128)(2,1)S(1)} %collective-permute-done.3.inner_ref, bf16[5,4,128,256]{3,2,1,0:T(8,128)(2,1)S(1)} %get-tuple-element.14.bands_ref, bf16[64,128]{1,0:T(8,128)(2,1)S(1)} %get-tuple-element.15.mix_ref, ...), custom_call_target="tpu_custom_call" | custom-call | tf_op jit(solution)/shard_map/pallas_call | solution.py:326
  (1 shorter events, 0.0 us)
Async XLA Ops:
  1.2 14.6 %collective-permute-start.1 = (bf16[8,2,32,128]{3,2,1,0:T(8,128)(2,1)S(1)}, bf16[8,2,32,128]{3,2,1,0:T(8,128)(2,1)S(1)}, u32[]{:S(2)}, u32[]{:S(2)}) collective-permute-start(bf16[8,2,32,128]{3,2,1,0:T(8,128)(2,1)S(1)} %shard_map.55.raw_ref), channel_id=1, source_target_pairs={{0,16},{16,32},{32,48},{48,64},{64,80},{80,96},{96,112},{112,128},... | collective-permute-start | bytes 393224 | tf_op jit(solution)/shard_map/ppermute | solution.py:340
  4.8 11.9 %collective-permute-start = (bf16[8,2,32,128]{3,2,1,0:T(8,128)(2,1)S(1)}, bf16[8,2,32,128]{3,2,1,0:T(8,128)(2,1)S(1)}, u32[]{:S(2)}, u32[]{:S(2)}) collective-permute-start(bf16[8,2,32,128]{3,2,1,0:T(8,128)(2,1)S(1)} %shard_map.55.raw_ref), channel_id=1, source_target_pairs={{16,0},{32,16},{48,32},{64,48},{80,64},{96,80},{112,96},{128,112},... | collective-permute-start | bytes 393224 | tf_op jit(solution)/shard_map/ppermute | solution.py:340
  16.7 11.8 %collective-permute-start.2 = (bf16[6,32,128]{2,1,0:T(8,128)(2,1)S(1)}, bf16[6,32,128]{2,1,0:T(8,128)(2,1)S(1)}, u32[]{:S(2)}, u32[]{:S(2)}) collective-permute-start(bf16[6,32,128]{2,1,0:T(8,128)(2,1)S(1)} %get-tuple-element.12), channel_id=1, source_target_pairs={{1,2},{3,4},{5,6},{7,8},{9,10},{11,12},{13,14},{2,1},{4,3},{6,5},{... | collective-permute-start | bytes 147464 | tf_op jit(solution)/shard_map/ppermute | solution.py:346
  21.3 7.2 %collective-permute-start.3 = (bf16[6,32,128]{2,1,0:T(8,128)(2,1)S(1)}, bf16[6,32,128]{2,1,0:T(8,128)(2,1)S(1)}, u32[]{:S(2)}, u32[]{:S(2)}) collective-permute-start(bf16[6,32,128]{2,1,0:T(8,128)(2,1)S(1)} %get-tuple-element.13), channel_id=1, source_target_pairs={{0,1},{2,3},{4,5},{6,7},{8,9},{10,11},{12,13},{14,15},{1,0},{3,2},... | collective-permute-start | bytes 147464 | tf_op jit(solution)/shard_map/ppermute | solution.py:346

commit v2 on v1

--- a/solution.py
+++ b/solution.py
@@ -130,9 +130,10 @@
         jnp.int32, shape, 0
     )
     nothing = jnp.zeros((LANES, LANES), BF16)
+    for e in range(3):
+        bands_ref[0, e, :LANES, LANES:] = nothing
+        bands_ref[2, e, LANES:, :LANES] = nothing
     for dq in range(depth // ROWS):
-        bands_ref[dq, 0, :, LANES:] = nothing
-        bands_ref[dq, 3, :, :LANES] = nothing
         for r in range(ROWS):
             at = dq * ROWS + r
             lines = [
@@ -146,9 +147,24 @@
             next_.append(jnp.zeros(shape, F32))
             for e in range(3):
                 block = jnp.where(later, same[e], next_[e]).astype(BF16)
-                span = slice(r * COLS, (r + 1) * COLS)
-                bands_ref[dq, e, span, :LANES] = block
-                bands_ref[dq, e + 1, span, LANES:] = block
+                for a in range(2):
+                    first = (dq + a) % 2 * LANES + r * COLS
+                    bands_ref[
+                        (dq + a) // 2, e, first : first + COLS, a * LANES : (a + 1) * LANES
+                    ] = block
+
+
+def render_all(raw_ref, bins_ref):
+    blocks, groups = raw_ref.shape[:2]
+
+    @pl.loop(0, blocks)
+    def _(k):
+        for q in range(groups):
+
+            def store(s, block):
+                bins_ref[k, s * BINS : (s + 1) * BINS, q * LANES : (q + 1) * LANES] = block
+
+            render(raw_ref[k, q], store)
 
 
 def own_kernel(
@@ -167,17 +183,7 @@
     sems,
 ):
     copies = fetch((footprint_hbm, gates_hbm), (footprint_ref, gates_ref), sems)
-    blocks, groups = raw_ref.shape[:2]
-
-    @pl.loop(0, blocks)
-    def _(k):
-        for q in range(groups):
-
-            def store(s, block):
-                own_ref[k, q, s * BINS : (s + 1) * BINS, :] = block
-
-            render(raw_ref[k, q], store)
-
+    render_all(raw_ref, own_ref)
     for copy in copies:
         copy.wait()
     weights(footprint_ref, taps_ref, fan_ref, turned_ref, bands_ref)
@@ -201,108 +207,74 @@
             target[at * groups : (at + 1) * groups] = source[k]
 
 
-def middle_kernel(
-    after_ref, own_ref, before_ref, bands_ref, mix_ref, part_ref, mid_ref, around_ref
+def around_kernel(
+    after_ref, own_ref, before_ref, bands_ref, mix_ref, ends_ref, mid_ref, below_ref, above_ref
 ):
-    blocks, groups = before_ref.shape[:2]
-    for at, source in enumerate((before_ref, after_ref)):
-
-        @pl.loop(0, blocks)
-        def _(k):
+    render_all(after_ref, below_ref)
+    render_all(before_ref, above_ref)
+    blocks, deep = own_ref.shape[:2]
+    nothing = jnp.zeros(own_ref.shape[1:], BF16)
+
+    def shifted_rows(source, e):
+        parts = [source[k] for k in range(max(e - 1, 0), min(blocks + e - 1, blocks))]
+        parts = [nothing] * (e == 0) + parts + [nothing] * (e == 2)
+        return jnp.concatenate(parts, axis=0)
+
+    left = jnp.concatenate(
+        [shifted_rows(source, e) for source in (above_ref, own_ref, below_ref) for e in range(3)],
+        axis=1,
+    )
+    right = bands_ref[...].reshape(9 * 2 * LANES, 2 * LANES)
+    total = jnp.dot(left, right, preferred_element_type=F32)
+    ends_ref[0] = total[:deep]
+    ends_ref[1] = total[(blocks - 1) * deep :]
+    smooth = total[deep : (blocks - 1) * deep].astype(BF16)
+    for k in range(blocks - 2):
+        mid_ref[k] = jnp.dot(
+            mix_ref[...], smooth[k * deep : (k + 1) * deep], preferred_element_type=F32
+        )
+
+
+def finish_kernel(
+    outer_ref, inner_ref, bands_ref, mix_ref, ends_ref, mid_ref, out_hbm, halo_ref, out_ref, sems
+):
+    spans = outer_ref.shape[0]
+    groups = spans // 3
+    for at, source in ((parity(), outer_ref), (1 - parity(), inner_ref)):
+
+        @pl.loop(0, 3)
+        def _(t):
             for q in range(groups):
 
                 def store(s, block):
-                    around_ref[at, k, q, s * BINS : (s + 1) * BINS, :] = block
-
-                render(source[k, q], store)
-
-    def piece(k, q):
-        if q < groups:
-            return around_ref[0, k, q]
-        if q < 2 * groups:
-            return own_ref[k, q - groups]
-        return around_ref[1, k, q - 2 * groups]
-
-    reach = bands_ref.shape[0]
-    pairs = blocks // 2
-    for pair in range(pairs):
-        inner = [j for j in range(4) if 0 <= 2 * pair + j - 1 < blocks]
-        total = None
-        for dq in range(reach):
-            left = jnp.concatenate(
-                [
-                    jnp.concatenate([piece(2 * pair + j - 1, a + dq) for j in inner], axis=1)
-                    for a in range(groups)
-                ],
-                axis=0,
-            )
-            right = bands_ref[dq, inner[0] : inner[-1] + 1].reshape(len(inner) * LANES, 2 * LANES)
-            term = jnp.dot(left, right, preferred_element_type=F32)
-            total = term if total is None else total + term
-        depth = total.shape[0] // groups
-        for side in range(2):
-            block = 2 * pair + side
-            lanes = slice(side * LANES, (side + 1) * LANES)
-            if block == 0:
-                part_ref[0] = total[:, lanes]
-            elif block == blocks - 1:
-                part_ref[1] = total[:, lanes]
-            else:
-                for a in range(groups):
-                    smooth = total[a * depth : (a + 1) * depth, lanes].astype(BF16)
-                    mid_ref[a, block - 1] = jnp.dot(
-                        mix_ref[...], smooth, preferred_element_type=F32
-                    )
-
-
-def finish_kernel(outer_ref, inner_ref, bands_ref, mix_ref, part_ref, mid_ref, out_ref, halo_ref):
-    spans = outer_ref.shape[0]
-    groups, mids = mid_ref.shape[:2]
-    reach = bands_ref.shape[0]
-
-    @pl.loop(0, spans)
-    def _(q):
-        for at, source in ((parity(), outer_ref), (1 - parity(), inner_ref)):
-
-            def store(s, block):
-                halo_ref[at, q, s * BINS : (s + 1) * BINS, :] = block
-
-            render(source[q], store)
-
-    ends = []
-    for at, (j, lanes) in enumerate(((0, slice(0, LANES)), (3, slice(LANES, 2 * LANES)))):
-        left = jnp.concatenate(
-            [
-                jnp.concatenate([halo_ref[at, a + dq] for dq in range(reach)], axis=1)
-                for a in range(groups)
-            ],
-            axis=0,
-        )
-        right = jnp.concatenate([bands_ref[dq, j, :, lanes] for dq in range(reach)], axis=0)
-        total = part_ref[at] + jnp.dot(left, right, preferred_element_type=F32)
-        depth = total.shape[0] // groups
-        ends.append(
-            [
-                jnp.dot(
-                    mix_ref[...],
-                    total[a * depth : (a + 1) * depth].astype(BF16),
-                    preferred_element_type=F32,
-                )
-                for a in range(groups)
-            ]
-        )
+                    halo_ref[at, t, s * BINS : (s + 1) * BINS, q * LANES : (q + 1) * LANES] = block
+
+                render(source[t * groups + q], store)
+
+    mixed = [mid_ref[k] for k in range(mid_ref.shape[0])]
+    for at, e in ((0, 0), (1, 2)):
+        left = jnp.concatenate([halo_ref[at, t] for t in range(3)], axis=1)
+        right = jnp.concatenate([bands_ref[t, e] for t in range(3)], axis=0)
+        smooth = ends_ref[at] + jnp.dot(left, right, preferred_element_type=F32)
+        block = jnp.dot(mix_ref[...], smooth.astype(BF16), preferred_element_type=F32)
+        mixed = [block] + mixed if at == 0 else mixed + [block]
     half = mix_ref.shape[0] // 2
     rows = groups * ROWS
     gates = out_ref.shape[0] // (2 * rows)
-    for a in range(groups):
-        for s in range(2):
-            span = slice(s * half, (s + 1) * half)
-            parts = [ends[0][a][span]]
-            parts += [mid_ref[a, k, span, :] for k in range(mids)]
-            parts += [ends[1][a][span]]
+    copies = []
+    for s in range(2):
+        for a in range(groups):
+            parts = [
+                block[s * half : (s + 1) * half, a * LANES : (a + 1) * LANES] for block in mixed
+            ]
             for r, block in enumerate(swap_groups(parts)):
                 first = s * gates * rows + a * ROWS + r
                 out_ref[pl.ds(first, gates, stride=rows), :] = block[:gates]
+        span = pl.ds(s * gates * rows, gates * rows)
+        copies.append(pltpu.make_async_copy(out_ref.at[span], out_hbm.at[span], sems.at[s]))
+        copies[-1].start()
+    for copy in copies:
+        copy.wait()
 
 
 def vmem(*shape, dtype=BF16):
@@ -317,8 +289,9 @@
     return [pltpu.with_memory_space_constraint(array, pltpu.VMEM) for array in arrays]
 
 
-def call(kernel, out, scratch, args, remote=(), flops=0, moved=0):
+def call(kernel, out, scratch, args, remote=(), flops=0, moved=0, place=pltpu.VMEM):
     whole = pl.BlockSpec(memory_space=pltpu.VMEM)
+    there = pl.BlockSpec(memory_space=place)
     many = isinstance(out, (list, tuple))
     if remote:
         scratch = scratch + [pltpu.VMEM(array.shape, array.dtype) for array in remote]
@@ -327,7 +300,7 @@
         kernel,
         out_shape=out,
         in_specs=[whole] * len(args) + [pl.BlockSpec(memory_space=pl.ANY)] * len(remote),
-        out_specs=[whole] * len(out) if many else whole,
+        out_specs=[there] * len(out) if many else there,
         scratch_shapes=scratch,
         compiler_params=pltpu.CompilerParams(vmem_limit_bytes=LIMIT),
         cost_estimate=pl.CostEstimate(flops=flops, bytes_accessed=moved, transcendentals=0),
@@ -350,7 +323,7 @@
     samples, layers, rows, width = layer_values.shape
     gates = depth_gate.shape[1]
     blocks, groups, channels = width // COLS, rows // ROWS, 2 * layers * samples
-    reach = (footprint.shape[0] + ROWS - 1) // ROWS
+    lines = -(-footprint.shape[0] // ROWS) * ROWS
     deep = samples * BINS
 
     raw = call(
@@ -365,14 +338,14 @@
     own, bands, mix = call(
         own_kernel,
         [
-            vmem(blocks, groups, deep, LANES),
-            vmem(reach, 4, LANES, 2 * LANES),
+            vmem(blocks, deep, groups * LANES),
+            vmem(3, 3, 2 * LANES, 2 * LANES),
             vmem(64, deep),
         ],
         [
             vmem(64, LANES, dtype=F32),
             vmem(64, 3 * LANES, dtype=F32),
-            vmem(reach * ROWS, 3 * LANES, dtype=F32),
+            vmem(lines, 3 * LANES, dtype=F32),
             vmem(64, deep, dtype=F32),
         ],
         (raw,),
@@ -388,13 +361,13 @@
     )
     outer = exchanged(outer, "cross", 1)
     inner = exchanged(inner, "cross", 0)
-    part, mid = call(
-        middle_kernel,
+    ends, mid = call(
+        around_kernel,
         [
-            vmem(2, groups * deep, LANES, dtype=F32),
-            vmem(groups, blocks - 2, 64, LANES, dtype=F32),
+            vmem(2, deep, groups * LANES, dtype=F32),
+            vmem(blocks - 2, 64, groups * LANES, dtype=F32),
         ],
-        [vmem(2, blocks, groups, deep, LANES)],
+        [vmem(blocks, deep, groups * LANES)] * 2,
         (after, own, before, bands, mix),
         flops=3_000_000_000,
         moved=4_000_000,
@@ -402,8 +375,13 @@
     out = call(
         finish_kernel,
         jax.ShapeDtypeStruct((samples * gates * rows, width), F32),
-        [vmem(2, 3 * groups, deep, LANES)],
-        (outer, inner, bands, mix, part, mid),
+        [
+            vmem(2, 3, deep, groups * LANES),
+            vmem(samples * gates * rows, width, dtype=F32),
+            pltpu.SemaphoreType.DMA((samples,)),
+        ],
+        (outer, inner, bands, mix, ends, mid),
+        place=pl.ANY,
     )
     return out.reshape(samples, gates, rows, width)
 

time: 30.9 us -> 29 us (0.939)
  the two profiles are of different devices: /device:TPU:7 before, /device:TPU:6 now
where the time goes in v2:
time: 29 us; the launch traced here: 28.5 us
  starting transfers between devices  19.5 us (67%)
  Pallas kernels  6.89 us (24%)
  waiting for transfers between devices  2.07 us (7%)
    ppermute x2, starting transfers between devices, shifted(): return lax.ppermute(array, axis, pairs)  13.6 us
    pallas_call x5, Pallas kernels, call(): pl.pallas_call(kernel, out_shape=out, in_specs=[whole] * len(args) + [pl....  6.89 us
    ppermute x2, starting transfers between devices, exchanged(): return lax.ppermute(array, axis, pairs + [(j, i) for i, j in pairs])  5.95 us
    ppermute x2, waiting for transfers between devices, shifted(): return lax.ppermute(array, axis, pairs)  1.47 us
    ppermute x2, waiting for transfers between devices, exchanged(): return lax.ppermute(array, axis, pairs + [(j, i) for i, j in pairs])  0.6 us
  transfers between devices with their start and end apart: 4, of which 3 were waited for; matrix products, arithmetic and copies ran while one was open for 0% of the time, Pallas kernels for 13%

profile of v2, /device:TPU:6, one launch (start us, length us, event | category | flops | bytes accessed | tf_op | source)
XLA Modules:
  0.0 28.5 jit_solution(16377070093376899313)
XLA Ops:
  0.0 1.2 %shard_map.55.raw_ref = bf16[8,2,32,128]{3,2,1,0:T(8,128)(2,1)S(1)} custom-call(s32[2,7,16,128]{3,2,1,0:T(8,128)} %bounds_hbm.1, s32[2,16,128]{2,1,0:T(8,128)} %count_hbm.1, bf16[2,8,16,128]{3,2,1,0:T(8,128)(2,1)} %values_hbm.1), custom_call_target="tpu_custom_call" | custom-call | tf_op jit(solution)/shard_map/pallas_call | solution.py:299
  1.2 3.8 %collective-permute-start.1 = (bf16[8,2,32,128]{3,2,1,0:T(8,128)(2,1)S(1)}, bf16[8,2,32,128]{3,2,1,0:T(8,128)(2,1)S(1)}, u32[]{:S(2)}, u32[]{:S(2)}) collective-permute-start(bf16[8,2,32,128]{3,2,1,0:T(8,128)(2,1)S(1)} %shard_map.55.raw_ref), channel_id=1, source_target_pairs={{0,16},{16,32},{32,48},{48,64},{64,80},{80,96},{96,112},{112,128},... | collective-permute-start | bytes 393224 | tf_op jit(solution)/shard_map/ppermute | solution.py:313
  5.1 9.8 %collective-permute-start = (bf16[8,2,32,128]{3,2,1,0:T(8,128)(2,1)S(1)}, bf16[8,2,32,128]{3,2,1,0:T(8,128)(2,1)S(1)}, u32[]{:S(2)}, u32[]{:S(2)}) collective-permute-start(bf16[8,2,32,128]{3,2,1,0:T(8,128)(2,1)S(1)} %shard_map.55.raw_ref), channel_id=1, source_target_pairs={{16,0},{32,16},{48,32},{64,48},{80,64},{96,80},{112,96},{128,112},... | collective-permute-start | bytes 393224 | tf_op jit(solution)/shard_map/ppermute | solution.py:313
  14.8 1.3 %shard_map.57 = (bf16[8,128,256]{2,1,0:T(8,128)(2,1)S(1)}, bf16[3,3,256,256]{3,2,1,0:T(8,128)(2,1)S(1)}, bf16[64,128]{1,0:T(8,128)(2,1)S(1)}) custom-call(bf16[8,2,32,128]{3,2,1,0:T(8,128)(2,1)S(1)} %shard_map.55.raw_ref, bf16[33,33]{1,0:T(8,128)(2,1)} %footprint_hbm.1, bf16[30,64]{1,0:T(8,128)(2,1)} %bitcast.2), custom_call_target="tpu_custom_call" | custom-call | flops 2000000000 | bytes 4000000 | tf_op jit(solution)/shard_map/pallas_call | solution.py:299
  16.1 0.3 %collective-permute-done.1.before_ref = bf16[8,2,32,128]{3,2,1,0:T(8,128)(2,1)S(1)} collective-permute-done((bf16[8,2,32,128]{3,2,1,0:T(8,128)(2,1)S(1)}, bf16[8,2,32,128]{3,2,1,0:T(8,128)(2,1)S(1)}, u32[]{:S(2)}, u32[]{:S(2)}) %collective-permute-start.1) | collective-permute-done | bytes 131104 | tf_op jit(solution)/shard_map/ppermute | solution.py:313
  16.4 1.2 %collective-permute-done.after_ref = bf16[8,2,32,128]{3,2,1,0:T(8,128)(2,1)S(1)} collective-permute-done((bf16[8,2,32,128]{3,2,1,0:T(8,128)(2,1)S(1)}, bf16[8,2,32,128]{3,2,1,0:T(8,128)(2,1)S(1)}, u32[]{:S(2)}, u32[]{:S(2)}) %collective-permute-start) | collective-permute-done | bytes 131104 | tf_op jit(solution)/shard_map/ppermute | solution.py:313
  17.6 4.0 %collective-permute-start.2 = (bf16[6,32,128]{2,1,0:T(8,128)(2,1)S(1)}, bf16[6,32,128]{2,1,0:T(8,128)(2,1)S(1)}, u32[]{:S(2)}, u32[]{:S(2)}) collective-permute-start(bf16[6,32,128]{2,1,0:T(8,128)(2,1)S(1)} %get-tuple-element.12), channel_id=1, source_target_pairs={{1,2},{3,4},{5,6},{7,8},{9,10},{11,12},{13,14},{2,1},{4,3},{6,5},{... | collective-permute-start | bytes 147464 | tf_op jit(solution)/shard_map/ppermute | solution.py:319
  21.6 1.9 %collective-permute-start.3 = (bf16[6,32,128]{2,1,0:T(8,128)(2,1)S(1)}, bf16[6,32,128]{2,1,0:T(8,128)(2,1)S(1)}, u32[]{:S(2)}, u32[]{:S(2)}) collective-permute-start(bf16[6,32,128]{2,1,0:T(8,128)(2,1)S(1)} %get-tuple-element.13), channel_id=1, source_target_pairs={{0,1},{2,3},{4,5},{6,7},{8,9},{10,11},{12,13},{14,15},{1,0},{3,2},... | collective-permute-start | bytes 147464 | tf_op jit(solution)/shard_map/ppermute | solution.py:319
  23.5 2.5 %shard_map.58 = (f32[2,128,256]{2,1,0:T(8,128)S(1)}, f32[6,64,256]{2,1,0:T(8,128)S(1)}) custom-call(bf16[8,2,32,128]{3,2,1,0:T(8,128)(2,1)S(1)} %collective-permute-done.after_ref, bf16[8,128,256]{2,1,0:T(8,128)(2,1)S(1)} %get-tuple-element.16.own_ref, bf16[8,2,32,128]{3,2,1,0:T(8,128)(2,1)S(1)} %collective-permute-done.1.before_ref, ...), custom_call_target="tpu_custom_call" | custom-call | flops 3000000000 | bytes 4000000 | tf_op jit(solution)/shard_map/pallas_call | solution.py:299
  26.0 0.6 %collective-permute-done.2.outer_ref = bf16[6,32,128]{2,1,0:T(8,128)(2,1)S(1)} collective-permute-done((bf16[6,32,128]{2,1,0:T(8,128)(2,1)S(1)}, bf16[6,32,128]{2,1,0:T(8,128)(2,1)S(1)}, u32[]{:S(2)}, u32[]{:S(2)}) %collective-permute-start.2) | collective-permute-done | bytes 49184 | tf_op jit(solution)/shard_map/ppermute | solution.py:319
  26.6 0.0 collective-permute-done.3.inner_ref
  26.6 2.0 %shard_map.59 = f32[960,128]{1,0:T(8,128)} custom-call(bf16[6,32,128]{2,1,0:T(8,128)(2,1)S(1)} %collective-permute-done.2.outer_ref, bf16[6,32,128]{2,1,0:T(8,128)(2,1)S(1)} %collective-permute-done.3.inner_ref, bf16[3,3,256,256]{3,2,1,0:T(8,128)(2,1)S(1)} %get-tuple-element.14.bands_ref, bf16[64,128]{1,0:T(8,128)(2,1)S(1)} %get-tuple-element.15.mix_ref, ...), custom_call_target="tpu_custom_call" | custom-call | tf_op jit(solution)/shard_map/pallas_call | solution.py:299
  (1 shorter events, 0.0 us)
Async XLA Ops:
  1.2 15.2 %collective-permute-start.1 = (bf16[8,2,32,128]{3,2,1,0:T(8,128)(2,1)S(1)}, bf16[8,2,32,128]{3,2,1,0:T(8,128)(2,1)S(1)}, u32[]{:S(2)}, u32[]{:S(2)}) collective-permute-start(bf16[8,2,32,128]{3,2,1,0:T(8,128)(2,1)S(1)} %shard_map.55.raw_ref), channel_id=1, source_target_pairs={{0,16},{16,32},{32,48},{48,64},{64,80},{80,96},{96,112},{112,128},... | collective-permute-start | bytes 393224 | tf_op jit(solution)/shard_map/ppermute | solution.py:313
  5.1 12.5 %collective-permute-start = (bf16[8,2,32,128]{3,2,1,0:T(8,128)(2,1)S(1)}, bf16[8,2,32,128]{3,2,1,0:T(8,128)(2,1)S(1)}, u32[]{:S(2)}, u32[]{:S(2)}) collective-permute-start(bf16[8,2,32,128]{3,2,1,0:T(8,128)(2,1)S(1)} %shard_map.55.raw_ref), channel_id=1, source_target_pairs={{16,0},{32,16},{48,32},{64,48},{80,64},{96,80},{112,96},{128,112},... | collective-permute-start | bytes 393224 | tf_op jit(solution)/shard_map/ppermute | solution.py:313
  17.6 9.0 %collective-permute-start.2 = (bf16[6,32,128]{2,1,0:T(8,128)(2,1)S(1)}, bf16[6,32,128]{2,1,0:T(8,128)(2,1)S(1)}, u32[]{:S(2)}, u32[]{:S(2)}) collective-permute-start(bf16[6,32,128]{2,1,0:T(8,128)(2,1)S(1)} %get-tuple-element.12), channel_id=1, source_target_pairs={{1,2},{3,4},{5,6},{7,8},{9,10},{11,12},{13,14},{2,1},{4,3},{6,5},{... | collective-permute-start | bytes 147464 | tf_op jit(solution)/shard_map/ppermute | solution.py:319
  21.6 5.0 %collective-permute-start.3 = (bf16[6,32,128]{2,1,0:T(8,128)(2,1)S(1)}, bf16[6,32,128]{2,1,0:T(8,128)(2,1)S(1)}, u32[]{:S(2)}, u32[]{:S(2)}) collective-permute-start(bf16[6,32,128]{2,1,0:T(8,128)(2,1)S(1)} %get-tuple-element.13), channel_id=1, source_target_pairs={{0,1},{2,3},{4,5},{6,7},{8,9},{10,11},{12,13},{14,15},{1,0},{3,2},... | collective-permute-start | bytes 147464 | tf_op jit(solution)/shard_map/ppermute | solution.py:319

commit v3 on v2

v3 whole, which is shorter than its diff:
```python
import functools

import jax
import jax.numpy as jnp
from jax import lax
from jax.experimental import pallas as pl
from jax.experimental.pallas import tpu as pltpu
from jax.sharding import PartitionSpec as P

ROWS = 8
COLS = 16
LANES = 128
BINS = 64
LIMIT = 40 * 1024 * 1024
BF16 = jnp.bfloat16
F32 = jnp.float32

NETWORK = (
    (0, 6), (2, 3), (4, 5),
    (0, 2), (1, 4), (3, 6),
    (0, 1), (2, 5), (3, 4),
    (1, 2), (4, 6),
    (2, 3), (4, 5),
    (1, 2), (3, 4), (5, 6),
)


def lane_group(shape):
    return lax.broadcasted_iota(jnp.int32, shape, len(shape) - 1) // COLS


def staggered(parts, sign):
    count = len(parts)
    group = lane_group(parts[0].shape)
    step = 1
    while step < count:
        chosen = (group // step) % 2 == 1
        parts = [
            jnp.where(chosen, parts[(m + sign * step) % count], parts[m]) for m in range(count)
        ]
        step *= 2
    return parts


def swap_groups(parts):
    count = len(parts)
    parts = [
        pltpu.roll(part, COLS * d, 1) if d else part for d, part in enumerate(staggered(parts, 1))
    ]
    return staggered([parts[-m % count] for m in range(count)], -1)


def pack_kernel(
    bounds_hbm,
    count_hbm,
    values_hbm,
    footprint_hbm,
    gates_hbm,
    raw_ref,
    footprint_ref,
    gates_ref,
    plane_ref,
    bounds_ref,
    count_ref,
    values_ref,
    sems,
):
    samples, layers = values_ref.shape[:2]
    rows = count_ref.shape[1]
    channels = 2 * layers
    copies = []
    for s in range(samples):
        for source, target in (
            (bounds_hbm, bounds_ref), (count_hbm, count_ref), (values_hbm, values_ref)
        ):
            copies.append((source.at[s], target.at[s]))
    copies += [(footprint_hbm, footprint_ref), (gates_hbm, gates_ref)]
    copies = [
        pltpu.make_async_copy(source, target, sems.at[at])
        for at, (source, target) in enumerate(copies)
    ]
    for copy in copies:
        copy.start()
    for s in range(samples):
        for copy in copies[3 * s : 3 * s + 3]:
            copy.wait()
        count = count_ref[s]
        keys = [
            jnp.where(k < count - 1, bounds_ref[s, k], BINS).astype(F32) for k in range(layers - 1)
        ]
        for low, high in NETWORK:
            keys[low], keys[high] = (
                jnp.minimum(keys[low], keys[high]),
                jnp.maximum(keys[low], keys[high]),
            )
        planes = keys + [jnp.zeros_like(keys[0])]
        planes += [values_ref[s, k].astype(F32) for k in range(layers)]
        for k, plane in enumerate(planes):
            first = (s * channels + k) * rows
            plane_ref[first : first + rows, :] = plane
        for q in range(rows // ROWS):
            parts = []
            for r in range(ROWS):
                first = s * channels * rows + q * ROWS + r
                parts.append(plane_ref[pl.ds(first, channels, stride=rows), :])
            for k, block in enumerate(swap_groups(parts)):
                raw_ref[k, q, s * channels : (s + 1) * channels, :] = block.astype(BF16)
    for copy in copies[3 * samples :]:
        copy.wait()


def render(raw):
    channels = raw.shape[0] // 2
    layers = channels // 2
    level = lax.broadcasted_iota(jnp.int32, (BINS, LANES), 0).astype(F32).astype(BF16)
    wide = raw.astype(F32)
    both = []
    for s in range(2):

        def row(k):
            line = wide[s * channels + k : s * channels + k + 1, :]
            line = jnp.broadcast_to(line, (16, LANES)).astype(BF16)
            return jnp.concatenate([line] * (BINS // 16), axis=0)

        bins = row(layers)
        for k in range(layers - 1):
            bins = jnp.where(row(k) <= level, row(layers + 1 + k), bins)
        both.append(bins)
    return jnp.concatenate(both, axis=0)


def weights(footprint_ref, taps_ref, fan_ref, turned_ref, bands_ref):
    side = footprint_ref.shape[0]
    taps_ref[...] = jnp.zeros_like(taps_ref)
    taps_ref[ROWS : ROWS + side, :side] = footprint_ref[...].astype(F32)
    shape = (LANES, 3 * LANES)
    dy = lax.broadcasted_iota(jnp.int32, shape, 0)
    lane = lax.broadcasted_iota(jnp.int32, shape, 1)
    pick = (dy == COLS * (lane // LANES) - lane % COLS).astype(F32).astype(BF16)
    fan_ref[...] = jnp.dot(taps_ref[...].astype(BF16), pick, preferred_element_type=F32)
    depth = turned_ref.shape[0]
    group = lane_group((depth, LANES))
    for e in range(3):
        lanes = slice(e * LANES, (e + 1) * LANES)
        turned = jnp.zeros((depth, LANES), F32)
        for r in range(ROWS):
            turned = jnp.where(group == r, fan_ref[ROWS - r : ROWS - r + depth, lanes], turned)
        turned_ref[:, lanes] = turned
    shape = (COLS, LANES)
    later = lax.broadcasted_iota(jnp.int32, shape, 1) % COLS >= lax.broadcasted_iota(
        jnp.int32, shape, 0
    )
    nothing = jnp.zeros((LANES, LANES), BF16)
    for e in range(3):
        bands_ref[0, e, :LANES, LANES:] = nothing
        bands_ref[2, e, LANES:, :LANES] = nothing
    for dq in range(depth // ROWS):
        for r in range(ROWS):
            at = dq * ROWS + r
            lines = [
                jnp.broadcast_to(turned_ref[at : at + 1, e * LANES : (e + 1) * LANES], shape)
                for e in range(3)
            ]
            same = [pltpu.roll(line, 0, 1, stride=1, stride_axis=0) for line in lines]
            next_ = [
                pltpu.roll(line, LANES - COLS, 1, stride=1, stride_axis=0) for line in lines[1:]
            ]
            next_.append(jnp.zeros(shape, F32))
            for e in range(3):
                block = jnp.where(later, same[e], next_[e]).astype(BF16)
                for a in range(2):
                    first = (dq + a) % 2 * LANES + r * COLS
                    bands_ref[
                        (dq + a) // 2, e, first : first + COLS, a * LANES : (a + 1) * LANES
                    ] = block


def render_all(raw_ref, bins_ref):
    blocks, groups = raw_ref.shape[:2]

    @pl.loop(0, blocks)
    def _(k):
        for q in range(groups):
            bins_ref[k, :, q * LANES : (q + 1) * LANES] = render(raw_ref[k, q])


def smoothed(bins_ref, bands_ref, t):
    blocks = bins_ref.shape[0]
    nothing = jnp.zeros(bins_ref.shape[1:], BF16)
    shifted_rows = []
    for e in range(3):
        parts = [bins_ref[k] for k in range(max(e - 1, 0), min(blocks + e - 1, blocks))]
        parts = [nothing] * (e == 0) + parts + [nothing] * (e == 2)
        shifted_rows.append(jnp.concatenate(parts, axis=0))
    right = bands_ref[t].reshape(3 * 2 * LANES, 2 * LANES)
    return jnp.dot(jnp.concatenate(shifted_rows, axis=1), right, preferred_element_type=F32)


def own_kernel(
    raw_ref,
    footprint_ref,
    gates_ref,
    total_ref,
    bands_ref,
    mix_ref,
    bins_ref,
    taps_ref,
    fan_ref,
    turned_ref,
    mixed_ref,
):
    render_all(raw_ref, bins_ref)
    weights(footprint_ref, taps_ref, fan_ref, turned_ref, bands_ref)
    gates, bins = gates_ref.shape
    half = mix_ref.shape[0] // 2
    mixed_ref[...] = jnp.zeros_like(mixed_ref)
    for s in range(2):
        mixed_ref[s * half : s * half + gates, s * bins : (s + 1) * bins] = gates_ref[...].astype(F32)
    mix_ref[...] = mixed_ref[...].astype(BF16)
    total_ref[...] = smoothed(bins_ref, bands_ref, 1)


def before_kernel(raw_ref, bands_ref, total_ref, more_ref, bins_ref):
    render_all(raw_ref, bins_ref)
    more_ref[...] = total_ref[...] + smoothed(bins_ref, bands_ref, 0)


def parity():
    return lax.rem(lax.axis_index("cross"), 2)


def edge_kernel(after_ref, raw_ref, before_ref, total_ref, outer_ref, inner_ref):
    groups = raw_ref.shape[1]
    end = raw_ref.shape[0] - 1
    for target, k in ((outer_ref, end * parity()), (inner_ref, end * (1 - parity()))):
        for at, source in enumerate((before_ref, raw_ref, after_ref)):
            target[at * groups : (at + 1) * groups] = source[k]


def after_kernel(raw_ref, bands_ref, mix_ref, total_ref, ends_ref, mid_ref, bins_ref):
    render_all(raw_ref, bins_ref)
    blocks, deep = bins_ref.shape[:2]
    total = total_ref[...] + smoothed(bins_ref, bands_ref, 2)
    ends_ref[0] = total[:deep]
    ends_ref[1] = total[(blocks - 1) * deep :]
    smooth = total[deep : (blocks - 1) * deep].astype(BF16)
    for k in range(blocks - 2):
        mid_ref[k] = jnp.dot(
            mix_ref[...], smooth[k * deep : (k + 1) * deep], preferred_element_type=F32
        )


def side_block(raw_ref, side, bands_ref, mix_ref, ends_ref):
    groups = raw_ref.shape[0] // 3
    left = jnp.concatenate([render(raw_ref[at]) for at in range(3 * groups)], axis=1)
    right = jnp.concatenate([bands_ref[t, 2 * side] for t in range(3)], axis=0)
    smooth = ends_ref[side] + jnp.dot(left, right, preferred_element_type=F32)
    return jnp.dot(mix_ref[...], smooth.astype(BF16), preferred_element_type=F32)


def finish_kernel(
    outer_ref, inner_ref, bands_ref, mix_ref, ends_ref, mid_ref, out_hbm, out_ref, sems
):
    groups = outer_ref.shape[0] // 3
    outer = side_block(outer_ref, parity(), bands_ref, mix_ref, ends_ref)
    inner = side_block(inner_ref, 1 - parity(), bands_ref, mix_ref, ends_ref)
    odd = parity() == 1
    mixed = [jnp.where(odd, inner, outer)]
    mixed += [mid_ref[k] for k in range(mid_ref.shape[0])]
    mixed += [jnp.where(odd, outer, inner)]
    half = mix_ref.shape[0] // 2
    rows = groups * ROWS
    gates = out_ref.shape[0] // (2 * rows)
    copies = []
    for s in range(2):
        for a in range(groups):
            for g in range(0, gates, 8):
                size = min(8, gates - g)
                parts = [
                    block[s * half + g : s * half + g + 8, a * LANES : (a + 1) * LANES]
                    for block in mixed
                ]
                for r, block in enumerate(swap_groups(parts)):
                    first = (s * gates + g) * rows + a * ROWS + r
                    out_ref[pl.ds(first, size, stride=rows), :] = block[:size]
        span = pl.ds(s * gates * rows, gates * rows)
        copies.append(pltpu.make_async_copy(out_ref.at[span], out_hbm.at[span], sems.at[s]))
        copies[-1].start()
    for copy in copies:
        copy.wait()


def vmem(*shape, dtype=BF16):
    return pltpu.VMEM(shape, dtype)


def far(*arrays):
    return [pltpu.with_memory_space_constraint(array, pltpu.HBM) for array in arrays]


def near(*arrays):
    return [pltpu.with_memory_space_constraint(array, pltpu.VMEM) for array in arrays]


def call(kernel, out, scratch, args, remote=(), place=pltpu.VMEM, alias=(), flops=0):
    whole = pl.BlockSpec(memory_space=pltpu.VMEM)
    there = pl.BlockSpec(memory_space=place)
    many = isinstance(out, (list, tuple))
    return pl.pallas_call(
        kernel,
        out_shape=out,
        in_specs=[whole] * len(args) + [pl.BlockSpec(memory_space=pl.ANY)] * len(remote),
        out_specs=[there] * len(out) if many else there,
        scratch_shapes=scratch,
        input_output_aliases=dict(alias),
        compiler_params=pltpu.CompilerParams(vmem_limit_bytes=LIMIT),
        cost_estimate=pl.CostEstimate(flops=flops, bytes_accessed=0, transcendentals=0),
    )(*near(*args), *far(*remote))


def shifted(array, axis, ahead):
    count = lax.axis_size(axis)
    pairs = [(i, i + 1) if ahead else (i + 1, i) for i in range(count - 1)]
    return lax.ppermute(array, axis, pairs)


def exchanged(array, axis, first):
    count = lax.axis_size(axis)
    pairs = [(i, i + 1) for i in range(first, count - 1, 2)]
    return lax.ppermute(array, axis, pairs + [(j, i) for i, j in pairs])


def local(interface_bins, layer_count, layer_values, footprint, depth_gate):
    samples, layers, rows, width = layer_values.shape
    gates = depth_gate.shape[1]
    blocks, groups, channels = width // COLS, rows // ROWS, 2 * layers * samples
    lines = -(-footprint.shape[0] // ROWS) * ROWS
    deep = samples * BINS

    raw, taps, turned = call(
        pack_kernel,
        [
            vmem(blocks, groups, channels, LANES),
            vmem(*footprint.shape),
            vmem(gates, BINS),
        ],
        [
            vmem(channels * rows, width, dtype=F32),
            vmem(*interface_bins.shape, dtype=jnp.int32),
            vmem(*layer_count.shape, dtype=jnp.int32),
            vmem(*layer_values.shape),
            pltpu.SemaphoreType.DMA((3 * samples + 2,)),
        ],
        (),
        remote=(interface_bins, layer_count, layer_values, footprint, depth_gate.T),
    )
    after = shifted(raw, "along", False)
    before = shifted(raw, "along", True)
    bins = vmem(blocks, deep, groups * LANES)
    sums = vmem(blocks * deep, groups * LANES, dtype=F32)
    total, bands, mix = call(
        own_kernel,
        [sums, vmem(3, 3, 2 * LANES, 2 * LANES), vmem(64, deep)],
        [
            bins,
            vmem(64, LANES, dtype=F32),
            vmem(64, 3 * LANES, dtype=F32),
            vmem(lines, 3 * LANES, dtype=F32),
            vmem(64, deep, dtype=F32),
        ],
        (raw, taps, turned),
        flops=2_000_000_000,
    )
    total = call(before_kernel, sums, [bins], (before, bands, total), alias={2: 0}, flops=10**9)
    outer, inner = call(
        edge_kernel,
        [vmem(3 * groups, channels, LANES)] * 2,
        [],
        (after, raw, before, total),
    )
    outer = exchanged(outer, "cross", 1)
    inner = exchanged(inner, "cross", 0)
    ends, mid = call(
        after_kernel,
        [
            vmem(2, deep, groups * LANES, dtype=F32),
            vmem(blocks - 2, 64, groups * LANES, dtype=F32),
        ],
        [bins],
        (after, bands, mix, total),
        flops=10**9,
    )
    out = call(
        finish_kernel,
        jax.ShapeDtypeStruct((samples * gates * rows, width), F32),
        [
            vmem(samples * gates * rows, width, dtype=F32),
            pltpu.SemaphoreType.DMA((samples,)),
        ],
        (outer, inner, bands, mix, ends, mid),
        place=pl.ANY,
    )
    return out.reshape(samples, gates, rows, width)


def solution(mesh):
    in_specs = (
        P(None, None, "along", "cross"),
        P(None, "along", "cross"),
        P(None, None, "along", "cross"),
        P(),
        P(),
    )
    out_specs = P(None, None, "along", "cross")
    return jax.shard_map(local, mesh=mesh, in_specs=in_specs, out_specs=out_specs, check_vma=False)
```

time: 29 us -> 28.4 us (0.979)
  waiting for transfers between devices: 2.07 us -> 1.54 us
  starting transfers between devices: 19.5 us -> 20 us
  Pallas kernels: 6.89 us -> 6.54 us
    ppermute x2, waiting for transfers between devices: 1.47 us -> 0.17 us  [shifted(): return lax.ppermute(array, axis, pairs)]
    ppermute x2, waiting for transfers between devices: 0.6 us -> 1.37 us  [exchanged(): return lax.ppermute(array, axis, pairs + [(j, i) for i, j in pairs])]
    ppermute x2, starting transfers between devices: 5.95 us -> 6.43 us  [exchanged(): return lax.ppermute(array, axis, pairs + [(j, i) for i, j in pairs])]
    pallas_call x5 -> x6, Pallas kernels: 6.89 us -> 6.54 us  [call(): pl.pallas_call(kernel, out_shape=out, in_specs=[whole] * len(args) + [pl....]
where the time goes in v3:
time: 28.4 us; the launch traced here: 28.2 us
  starting transfers between devices  20 us (70%)
  Pallas kernels  6.54 us (23%)
  waiting for transfers between devices  1.54 us (5%)
    ppermute x2, starting transfers between devices, shifted(): return lax.ppermute(array, axis, pairs)  13.6 us
    pallas_call x6, Pallas kernels, call(): pl.pallas_call(kernel, out_shape=out, in_specs=[whole] * len(args) + [pl....  6.54 us
    ppermute x2, starting transfers between devices, exchanged(): return lax.ppermute(array, axis, pairs + [(j, i) for i, j in pairs])  6.43 us
    ppermute x2, waiting for transfers between devices, exchanged(): return lax.ppermute(array, axis, pairs + [(j, i) for i, j in pairs])  1.37 us
  transfers between devices with their start and end apart: 4, of which 3 were waited for; matrix products, arithmetic and copies ran while one was open for 0% of the time, Pallas kernels for 13%

profile of v3, /device:TPU:6, one launch (start us, length us, event | category | flops | bytes accessed | tf_op | source)
XLA Modules:
  0.0 28.2 jit_solution(10912334027021663099)
XLA Ops:
  0.0 1.2 %shard_map.55 = (bf16[8,2,32,128]{3,2,1,0:T(8,128)(2,1)S(1)}, bf16[33,33]{1,0:T(8,128)(2,1)S(1)}, bf16[30,64]{1,0:T(8,128)(2,1)S(1)}) custom-call(s32[2,7,16,128]{3,2,1,0:T(8,128)} %bounds_hbm.1, s32[2,16,128]{2,1,0:T(8,128)} %count_hbm.1, bf16[2,8,16,128]{3,2,1,0:T(8,128)(2,1)} %values_hbm.1, bf16[33,33]{1,0:T(8,128)(2,1)} %footprint_hbm.1, ...), custom_call_target="tpu_custom_call" | custom-call | tf_op jit(solution)/shard_map/pallas_call | solution.py:309
  1.2 3.8 %collective-permute-start.1 = (bf16[8,2,32,128]{3,2,1,0:T(8,128)(2,1)S(1)}, bf16[8,2,32,128]{3,2,1,0:T(8,128)(2,1)S(1)}, u32[]{:S(2)}, u32[]{:S(2)}) collective-permute-start(bf16[8,2,32,128]{3,2,1,0:T(8,128)(2,1)S(1)} %get-tuple-element.15.raw_ref), channel_id=1, source_target_pairs={{0,16},{16,32},{32,48},{48,64},{64,80},{80,96},{96,112},{112,128},... | collective-permute-start | bytes 393224 | tf_op jit(solution)/shard_map/ppermute | solution.py:324
  5.0 9.8 %collective-permute-start = (bf16[8,2,32,128]{3,2,1,0:T(8,128)(2,1)S(1)}, bf16[8,2,32,128]{3,2,1,0:T(8,128)(2,1)S(1)}, u32[]{:S(2)}, u32[]{:S(2)}) collective-permute-start(bf16[8,2,32,128]{3,2,1,0:T(8,128)(2,1)S(1)} %get-tuple-element.15.raw_ref), channel_id=1, source_target_pairs={{16,0},{32,16},{48,32},{64,48},{80,64},{96,80},{112,96},{128,112},... | collective-permute-start | bytes 393224 | tf_op jit(solution)/shard_map/ppermute | solution.py:324
  14.8 1.5 %shard_map.56 = (f32[1024,256]{1,0:T(8,128)S(1)}, bf16[3,3,256,256]{3,2,1,0:T(8,128)(2,1)S(1)}, bf16[64,128]{1,0:T(8,128)(2,1)S(1)}) custom-call(bf16[8,2,32,128]{3,2,1,0:T(8,128)(2,1)S(1)} %get-tuple-element.15.raw_ref, bf16[33,33]{1,0:T(8,128)(2,1)S(1)} %get-tuple-element.16.footprint_ref, bf16[30,64]{1,0:T(8,128)(2,1)S(1)} %get-tuple-element.17.gates_ref), custom_call_target="tpu_custom_call" | custom-call | flops 2000000000 | tf_op jit(solution)/shard_map/pallas_call | solution.py:309
  16.3 0.1 collective-permute-done.1.raw_ref.before_ref
  16.4 1.1 %shard_map.57.total_ref = f32[1024,256]{1,0:T(8,128)S(1)} custom-call(bf16[8,2,32,128]{3,2,1,0:T(8,128)(2,1)S(1)} %collective-permute-done.1.raw_ref.before_ref, bf16[3,3,256,256]{3,2,1,0:T(8,128)(2,1)S(1)} %get-tuple-element.18.bands_ref, f32[1024,256]{1,0:T(8,128)S(1)} %get-tuple-element.19.total_ref), custom_call_target="tpu_custom_call", output_to_operand_aliasing={{}: (2, {})} | custom-call | flops 1000000000 | tf_op jit(solution)/shard_map/pallas_call | solution.py:309
  17.4 0.1 collective-permute-done.after_ref.raw_ref
  17.6 4.5 %collective-permute-start.2 = (bf16[6,32,128]{2,1,0:T(8,128)(2,1)S(1)}, bf16[6,32,128]{2,1,0:T(8,128)(2,1)S(1)}, u32[]{:S(2)}, u32[]{:S(2)}) collective-permute-start(bf16[6,32,128]{2,1,0:T(8,128)(2,1)S(1)} %get-tuple-element.20), channel_id=1, source_target_pairs={{1,2},{3,4},{5,6},{7,8},{9,10},{11,12},{13,14},{2,1},{4,3},{6,5},{... | collective-permute-start | bytes 147464 | tf_op jit(solution)/shard_map/ppermute | solution.py:330
  22.1 1.9 %collective-permute-start.3 = (bf16[6,32,128]{2,1,0:T(8,128)(2,1)S(1)}, bf16[6,32,128]{2,1,0:T(8,128)(2,1)S(1)}, u32[]{:S(2)}, u32[]{:S(2)}) collective-permute-start(bf16[6,32,128]{2,1,0:T(8,128)(2,1)S(1)} %get-tuple-element.21), channel_id=1, source_target_pairs={{0,1},{2,3},{4,5},{6,7},{8,9},{10,11},{12,13},{14,15},{1,0},{3,2},... | collective-permute-start | bytes 147464 | tf_op jit(solution)/shard_map/ppermute | solution.py:330
  24.0 1.2 %shard_map.59 = (f32[2,128,256]{2,1,0:T(8,128)S(1)}, f32[6,64,256]{2,1,0:T(8,128)S(1)}) custom-call(bf16[8,2,32,128]{3,2,1,0:T(8,128)(2,1)S(1)} %collective-permute-done.after_ref.raw_ref, bf16[3,3,256,256]{3,2,1,0:T(8,128)(2,1)S(1)} %get-tuple-element.18.bands_ref, bf16[64,128]{1,0:T(8,128)(2,1)S(1)} %get-tuple-element.22.mix_ref, ...), custom_call_target="tpu_custom_call" | custom-call | flops 1000000000 | tf_op jit(solution)/shard_map/pallas_call | solution.py:309
  25.2 1.4 %collective-permute-done.2.outer_ref = bf16[6,32,128]{2,1,0:T(8,128)(2,1)S(1)} collective-permute-done((bf16[6,32,128]{2,1,0:T(8,128)(2,1)S(1)}, bf16[6,32,128]{2,1,0:T(8,128)(2,1)S(1)}, u32[]{:S(2)}, u32[]{:S(2)}) %collective-permute-start.2) | collective-permute-done | bytes 49184 | tf_op jit(solution)/shard_map/ppermute | solution.py:330
  26.6 0.0 collective-permute-done.3.inner_ref
  26.6 1.6 %shard_map.60 = f32[960,128]{1,0:T(8,128)} custom-call(bf16[6,32,128]{2,1,0:T(8,128)(2,1)S(1)} %collective-permute-done.2.outer_ref, bf16[6,32,128]{2,1,0:T(8,128)(2,1)S(1)} %collective-permute-done.3.inner_ref, bf16[3,3,256,256]{3,2,1,0:T(8,128)(2,1)S(1)} %get-tuple-element.18.bands_ref, bf16[64,128]{1,0:T(8,128)(2,1)S(1)} %get-tuple-element.22.mix_ref, ...), custom_call_target="tpu_custom_call" | custom-call | tf_op jit(solution)/shard_map/pallas_call | solution.py:309
  (1 shorter events, 0.0 us)
Async XLA Ops:
  1.2 15.2 %collective-permute-start.1 = (bf16[8,2,32,128]{3,2,1,0:T(8,128)(2,1)S(1)}, bf16[8,2,32,128]{3,2,1,0:T(8,128)(2,1)S(1)}, u32[]{:S(2)}, u32[]{:S(2)}) collective-permute-start(bf16[8,2,32,128]{3,2,1,0:T(8,128)(2,1)S(1)} %get-tuple-element.15.raw_ref), channel_id=1, source_target_pairs={{0,16},{16,32},{32,48},{48,64},{64,80},{80,96},{96,112},{112,128},... | collective-permute-start | bytes 393224 | tf_op jit(solution)/shard_map/ppermute | solution.py:324
  5.0 12.5 %collective-permute-start = (bf16[8,2,32,128]{3,2,1,0:T(8,128)(2,1)S(1)}, bf16[8,2,32,128]{3,2,1,0:T(8,128)(2,1)S(1)}, u32[]{:S(2)}, u32[]{:S(2)}) collective-permute-start(bf16[8,2,32,128]{3,2,1,0:T(8,128)(2,1)S(1)} %get-tuple-element.15.raw_ref), channel_id=1, source_target_pairs={{16,0},{32,16},{48,32},{64,48},{80,64},{96,80},{112,96},{128,112},... | collective-permute-start | bytes 393224 | tf_op jit(solution)/shard_map/ppermute | solution.py:324
  17.6 9.0 %collective-permute-start.2 = (bf16[6,32,128]{2,1,0:T(8,128)(2,1)S(1)}, bf16[6,32,128]{2,1,0:T(8,128)(2,1)S(1)}, u32[]{:S(2)}, u32[]{:S(2)}) collective-permute-start(bf16[6,32,128]{2,1,0:T(8,128)(2,1)S(1)} %get-tuple-element.20), channel_id=1, source_target_pairs={{1,2},{3,4},{5,6},{7,8},{9,10},{11,12},{13,14},{2,1},{4,3},{6,5},{... | collective-permute-start | bytes 147464 | tf_op jit(solution)/shard_map/ppermute | solution.py:330
  22.1 4.5 %collective-permute-start.3 = (bf16[6,32,128]{2,1,0:T(8,128)(2,1)S(1)}, bf16[6,32,128]{2,1,0:T(8,128)(2,1)S(1)}, u32[]{:S(2)}, u32[]{:S(2)}) collective-permute-start(bf16[6,32,128]{2,1,0:T(8,128)(2,1)S(1)} %get-tuple-element.21), channel_id=1, source_target_pairs={{0,1},{2,3},{4,5},{6,7},{8,9},{10,11},{12,13},{14,15},{1,0},{3,2},... | collective-permute-start | bytes 147464 | tf_op jit(solution)/shard_map/ppermute | solution.py:330

commit v4 on v3

--- a/solution.py
+++ b/solution.py
@@ -220,34 +220,48 @@
     total_ref[...] = smoothed(bins_ref, bands_ref, 1)
 
 
-def before_kernel(raw_ref, bands_ref, total_ref, more_ref, bins_ref):
-    render_all(raw_ref, bins_ref)
-    more_ref[...] = total_ref[...] + smoothed(bins_ref, bands_ref, 0)
+def odd_row():
+    return lax.rem(lax.axis_index("along"), 2)
 
 
 def parity():
     return lax.rem(lax.axis_index("cross"), 2)
 
 
-def edge_kernel(after_ref, raw_ref, before_ref, total_ref, outer_ref, inner_ref):
+def first_kernel(raw_ref, bands_ref, total_ref, more_ref, bins_ref):
+    render_all(raw_ref, bins_ref)
+    more_ref[...] = total_ref[...] + smoothed(bins_ref, bands_ref, 2 * (1 - odd_row()))
+
+
+def edge_kernel(second_ref, raw_ref, late_ref, first_ref, total_ref, outer_ref, inner_ref):
     groups = raw_ref.shape[1]
     end = raw_ref.shape[0] - 1
+    odd = odd_row() == 1
     for target, k in ((outer_ref, end * parity()), (inner_ref, end * (1 - parity()))):
-        for at, source in enumerate((before_ref, raw_ref, after_ref)):
-            target[at * groups : (at + 1) * groups] = source[k]
-
-
-def after_kernel(raw_ref, bands_ref, mix_ref, total_ref, ends_ref, mid_ref, bins_ref):
-    render_all(raw_ref, bins_ref)
+        near_rows = first_ref[k] + late_ref[k]
+        far_rows = second_ref[k]
+        target[:groups] = jnp.where(odd, near_rows, far_rows)
+        target[groups : 2 * groups] = raw_ref[k]
+        target[2 * groups :] = jnp.where(odd, far_rows, near_rows)
+
+
+def second_kernel(
+    second_ref, late_ref, bands_ref, mix_ref, total_ref, ends_ref, mid_ref, bins_ref, sum_ref
+):
+    render_all(second_ref, bins_ref)
     blocks, deep = bins_ref.shape[:2]
-    total = total_ref[...] + smoothed(bins_ref, bands_ref, 2)
-    ends_ref[0] = total[:deep]
-    ends_ref[1] = total[(blocks - 1) * deep :]
-    smooth = total[deep : (blocks - 1) * deep].astype(BF16)
+    sum_ref[...] = total_ref[...] + smoothed(bins_ref, bands_ref, 2 * odd_row())
+
+    @pl.when(is_late())
+    def _():
+        render_all(late_ref, bins_ref)
+        sum_ref[...] += smoothed(bins_ref, bands_ref, 2 * (1 - odd_row()))
+
+    ends_ref[0] = sum_ref[:deep]
+    ends_ref[1] = sum_ref[(blocks - 1) * deep :]
     for k in range(blocks - 2):
-        mid_ref[k] = jnp.dot(
-            mix_ref[...], smooth[k * deep : (k + 1) * deep], preferred_element_type=F32
-        )
+        smooth = sum_ref[(k + 1) * deep : (k + 2) * deep].astype(BF16)
+        mid_ref[k] = jnp.dot(mix_ref[...], smooth, preferred_element_type=F32)
 
 
 def side_block(raw_ref, side, bands_ref, mix_ref, ends_ref):
@@ -318,16 +332,22 @@
     )(*near(*args), *far(*remote))
 
 
-def shifted(array, axis, ahead):
-    count = lax.axis_size(axis)
-    pairs = [(i, i + 1) if ahead else (i + 1, i) for i in range(count - 1)]
-    return lax.ppermute(array, axis, pairs)
-
-
-def exchanged(array, axis, first):
-    count = lax.axis_size(axis)
-    pairs = [(i, i + 1) for i in range(first, count - 1, 2)]
+def late_pair(count):
+    return (count // 2 - 2, count // 2 - 1) if count % 4 == 0 else None
+
+
+def is_late():
+    pair = late_pair(lax.axis_size("along"))
+    here = lax.axis_index("along")
+    return (here == pair[0]) | (here == pair[1]) if pair else here < 0
+
+
+def swapped(array, axis, pairs):
     return lax.ppermute(array, axis, pairs + [(j, i) for i, j in pairs])
+
+
+def pairs_from(first, count):
+    return [(i, i + 1) for i in range(first, count - 1, 2)]
 
 
 def local(interface_bins, layer_count, layer_values, footprint, depth_gate):
@@ -354,8 +374,11 @@
         (),
         remote=(interface_bins, layer_count, layer_values, footprint, depth_gate.T),
     )
-    after = shifted(raw, "along", False)
-    before = shifted(raw, "along", True)
+    count = lax.axis_size("along")
+    pair = late_pair(count)
+    first = swapped(raw, "along", [p for p in pairs_from(0, count) if p != pair])
+    second = swapped(raw, "along", pairs_from(1, count))
+    late = swapped(raw, "along", [pair]) if pair else jnp.zeros_like(raw)
     bins = vmem(blocks, deep, groups * LANES)
     sums = vmem(blocks * deep, groups * LANES, dtype=F32)
     total, bands, mix = call(
@@ -371,23 +394,24 @@
         (raw, taps, turned),
         flops=2_000_000_000,
     )
-    total = call(before_kernel, sums, [bins], (before, bands, total), alias={2: 0}, flops=10**9)
+    total = call(first_kernel, sums, [bins], (first, bands, total), alias={2: 0}, flops=10**9)
     outer, inner = call(
         edge_kernel,
         [vmem(3 * groups, channels, LANES)] * 2,
         [],
-        (after, raw, before, total),
-    )
-    outer = exchanged(outer, "cross", 1)
-    inner = exchanged(inner, "cross", 0)
+        (second, raw, late, first, total),
+    )
+    wide = lax.axis_size("cross")
+    outer = swapped(outer, "cross", pairs_from(1, wide))
+    inner = swapped(inner, "cross", pairs_from(0, wide))
     ends, mid = call(
-        after_kernel,
+        second_kernel,
         [
             vmem(2, deep, groups * LANES, dtype=F32),
             vmem(blocks - 2, 64, groups * LANES, dtype=F32),
         ],
-        [bins],
-        (after, bands, mix, total),
+        [bins, sums],
+        (second, late, bands, mix, total),
         flops=10**9,
     )
     out = call(

time: 28.4 us -> 28 us (0.986)
  starting transfers between devices: 20 us -> 19.3 us
    ppermute x4 -> x5, starting transfers between devices: 20 us -> 19.3 us  [swapped(): return lax.ppermute(array, axis, pairs + [(j, i) for i, j in pairs])]
    ppermute x4 -> x5, waiting for transfers between devices: 1.54 us -> 1.77 us  [swapped(): return lax.ppermute(array, axis, pairs + [(j, i) for i, j in pairs])]
  transfers between devices with their start and end apart: 4 -> 5, of which waited for: 3 -> 2; matrix products, arithmetic and copies ran while one was open for 0% -> 0% of each run, Pallas kernels for 13% -> 14%
where the time goes in v4:
time: 28 us; the launch traced here: 27.8 us
  starting transfers between devices  19.3 us (69%)
  Pallas kernels  6.64 us (24%)
  waiting for transfers between devices  1.77 us (6%)
    ppermute x5, starting transfers between devices, swapped(): return lax.ppermute(array, axis, pairs + [(j, i) for i, j in pairs])  19.3 us
    pallas_call x6, Pallas kernels, call(): pl.pallas_call(kernel, out_shape=out, in_specs=[whole] * len(args) + [pl....  6.64 us
    ppermute x5, waiting for transfers between devices, swapped(): return lax.ppermute(array, axis, pairs + [(j, i) for i, j in pairs])  1.77 us
  transfers between devices with their start and end apart: 5, of which 2 were waited for; matrix products, arithmetic and copies ran while one was open for 0% of the time, Pallas kernels for 14%

profile of v4, /device:TPU:6, one launch (start us, length us, event | category | flops | bytes accessed | tf_op | source)
XLA Modules:
  0.0 27.8 jit_solution(10416676604016911137)
XLA Ops:
  0.0 1.2 %shard_map.55 = (bf16[8,2,32,128]{3,2,1,0:T(8,128)(2,1)S(1)}, bf16[33,33]{1,0:T(8,128)(2,1)S(1)}, bf16[30,64]{1,0:T(8,128)(2,1)S(1)}) custom-call(s32[2,7,16,128]{3,2,1,0:T(8,128)} %bounds_hbm.1, s32[2,16,128]{2,1,0:T(8,128)} %count_hbm.1, bf16[2,8,16,128]{3,2,1,0:T(8,128)(2,1)} %values_hbm.1, bf16[33,33]{1,0:T(8,128)(2,1)} %footprint_hbm.1, ...), custom_call_target="tpu_custom_call" | custom-call | tf_op jit(solution)/shard_map/pallas_call | solution.py:323
  1.2 3.8 %collective-permute-start.2 = (bf16[8,2,32,128]{3,2,1,0:T(8,128)(2,1)S(1)}, bf16[8,2,32,128]{3,2,1,0:T(8,128)(2,1)S(1)}, u32[]{:S(2)}, u32[]{:S(2)}) collective-permute-start(bf16[8,2,32,128]{3,2,1,0:T(8,128)(2,1)S(1)} %get-tuple-element.15.raw_ref), channel_id=1, source_target_pairs={{0,16},{32,48},{64,80},{96,112},{128,144},{160,176},{192,208},{256... | collective-permute-start | bytes 393224 | tf_op jit(solution)/shard_map/ppermute | solution.py:346
  5.0 8.5 %collective-permute-start = (bf16[8,2,32,128]{3,2,1,0:T(8,128)(2,1)S(1)}, bf16[8,2,32,128]{3,2,1,0:T(8,128)(2,1)S(1)}, u32[]{:S(2)}, u32[]{:S(2)}) collective-permute-start(bf16[8,2,32,128]{3,2,1,0:T(8,128)(2,1)S(1)} %get-tuple-element.15.raw_ref), channel_id=1, source_target_pairs={{16,32},{48,64},{80,96},{112,128},{144,160},{176,192},{208,224},{2... | collective-permute-start | bytes 393224 | tf_op jit(solution)/shard_map/ppermute | solution.py:346
  13.6 0.7 %collective-permute-start.1 = (bf16[8,2,32,128]{3,2,1,0:T(8,128)(2,1)S(1)}, bf16[8,2,32,128]{3,2,1,0:T(8,128)(2,1)S(1)}, u32[]{:S(2)}, u32[]{:S(2)}) collective-permute-start(bf16[8,2,32,128]{3,2,1,0:T(8,128)(2,1)S(1)} %get-tuple-element.15.raw_ref), channel_id=1, source_target_pairs={{224,240},{240,224},{225,241},{241,225},{226,242},{242,226},{227,2... | collective-permute-start | bytes 393224 | tf_op jit(solution)/shard_map/ppermute | solution.py:346
  14.2 1.5 %shard_map.56 = (f32[1024,256]{1,0:T(8,128)S(1)}, bf16[3,3,256,256]{3,2,1,0:T(8,128)(2,1)S(1)}, bf16[64,128]{1,0:T(8,128)(2,1)S(1)}) custom-call(bf16[8,2,32,128]{3,2,1,0:T(8,128)(2,1)S(1)} %get-tuple-element.15.raw_ref, bf16[33,33]{1,0:T(8,128)(2,1)S(1)} %get-tuple-element.16.footprint_ref, bf16[30,64]{1,0:T(8,128)(2,1)S(1)} %get-tuple-element.17.gates_ref), custom_call_target="tpu_custom_call" | custom-call | flops 2000000000 | tf_op jit(solution)/shard_map/pallas_call | solution.py:323
  15.7 0.0 collective-permute-done.2.raw_ref.first_ref
  15.7 1.1 %shard_map.57.total_ref = f32[1024,256]{1,0:T(8,128)S(1)} custom-call(bf16[8,2,32,128]{3,2,1,0:T(8,128)(2,1)S(1)} %collective-permute-done.2.raw_ref.first_ref, bf16[3,3,256,256]{3,2,1,0:T(8,128)(2,1)S(1)} %get-tuple-element.18.bands_ref, f32[1024,256]{1,0:T(8,128)S(1)} %get-tuple-element.19.total_ref), custom_call_target="tpu_custom_call", output_to_operand_aliasing={{}: (2, {})} | custom-call | flops 1000000000 | tf_op jit(solution)/shard_map/pallas_call | solution.py:323
  16.8 0.3 %collective-permute-done.second_ref = bf16[8,2,32,128]{3,2,1,0:T(8,128)(2,1)S(1)} collective-permute-done((bf16[8,2,32,128]{3,2,1,0:T(8,128)(2,1)S(1)}, bf16[8,2,32,128]{3,2,1,0:T(8,128)(2,1)S(1)}, u32[]{:S(2)}, u32[]{:S(2)}) %collective-permute-start) | collective-permute-done | bytes 131104 | tf_op jit(solution)/shard_map/ppermute | solution.py:346
  17.1 0.0 collective-permute-done.1.late_ref
  17.2 4.4 %collective-permute-start.3 = (bf16[6,32,128]{2,1,0:T(8,128)(2,1)S(1)}, bf16[6,32,128]{2,1,0:T(8,128)(2,1)S(1)}, u32[]{:S(2)}, u32[]{:S(2)}) collective-permute-start(bf16[6,32,128]{2,1,0:T(8,128)(2,1)S(1)} %get-tuple-element.20), channel_id=1, source_target_pairs={{1,2},{3,4},{5,6},{7,8},{9,10},{11,12},{13,14},{2,1},{4,3},{6,5},{... | collective-permute-start | bytes 147464 | tf_op jit(solution)/shard_map/ppermute | solution.py:346
  21.5 1.9 %collective-permute-start.4 = (bf16[6,32,128]{2,1,0:T(8,128)(2,1)S(1)}, bf16[6,32,128]{2,1,0:T(8,128)(2,1)S(1)}, u32[]{:S(2)}, u32[]{:S(2)}) collective-permute-start(bf16[6,32,128]{2,1,0:T(8,128)(2,1)S(1)} %get-tuple-element.21), channel_id=1, source_target_pairs={{0,1},{2,3},{4,5},{6,7},{8,9},{10,11},{12,13},{14,15},{1,0},{3,2},... | collective-permute-start | bytes 147464 | tf_op jit(solution)/shard_map/ppermute | solution.py:346
  23.5 1.3 %shard_map.59 = (f32[2,128,256]{2,1,0:T(8,128)S(1)}, f32[6,64,256]{2,1,0:T(8,128)S(1)}) custom-call(bf16[8,2,32,128]{3,2,1,0:T(8,128)(2,1)S(1)} %collective-permute-done.second_ref, bf16[8,2,32,128]{3,2,1,0:T(8,128)(2,1)S(1)} %collective-permute-done.1.late_ref, bf16[3,3,256,256]{3,2,1,0:T(8,128)(2,1)S(1)} %get-tuple-element.18.bands_ref, ...), custom_call_target="tpu_custom_call" | custom-call | flops 1000000000 | tf_op jit(solution)/shard_map/pallas_call | solution.py:323
  24.7 1.5 %collective-permute-done.3.outer_ref = bf16[6,32,128]{2,1,0:T(8,128)(2,1)S(1)} collective-permute-done((bf16[6,32,128]{2,1,0:T(8,128)(2,1)S(1)}, bf16[6,32,128]{2,1,0:T(8,128)(2,1)S(1)}, u32[]{:S(2)}, u32[]{:S(2)}) %collective-permute-start.3) | collective-permute-done | bytes 49184 | tf_op jit(solution)/shard_map/ppermute | solution.py:346
  26.2 0.0 collective-permute-done.4.inner_ref
  26.2 1.6 %shard_map.60 = f32[960,128]{1,0:T(8,128)} custom-call(bf16[6,32,128]{2,1,0:T(8,128)(2,1)S(1)} %collective-permute-done.3.outer_ref, bf16[6,32,128]{2,1,0:T(8,128)(2,1)S(1)} %collective-permute-done.4.inner_ref, bf16[3,3,256,256]{3,2,1,0:T(8,128)(2,1)S(1)} %get-tuple-element.18.bands_ref, bf16[64,128]{1,0:T(8,128)(2,1)S(1)} %get-tuple-element.22.mix_ref, ...), custom_call_target="tpu_custom_call" | custom-call | tf_op jit(solution)/shard_map/pallas_call | solution.py:323
  (1 shorter events, 0.0 us)
Async XLA Ops:
  1.2 14.5 %collective-permute-start.2 = (bf16[8,2,32,128]{3,2,1,0:T(8,128)(2,1)S(1)}, bf16[8,2,32,128]{3,2,1,0:T(8,128)(2,1)S(1)}, u32[]{:S(2)}, u32[]{:S(2)}) collective-permute-start(bf16[8,2,32,128]{3,2,1,0:T(8,128)(2,1)S(1)} %get-tuple-element.15.raw_ref), channel_id=1, source_target_pairs={{0,16},{32,48},{64,80},{96,112},{128,144},{160,176},{192,208},{256... | collective-permute-start | bytes 393224 | tf_op jit(solution)/shard_map/ppermute | solution.py:346
  5.0 12.1 %collective-permute-start = (bf16[8,2,32,128]{3,2,1,0:T(8,128)(2,1)S(1)}, bf16[8,2,32,128]{3,2,1,0:T(8,128)(2,1)S(1)}, u32[]{:S(2)}, u32[]{:S(2)}) collective-permute-start(bf16[8,2,32,128]{3,2,1,0:T(8,128)(2,1)S(1)} %get-tuple-element.15.raw_ref), channel_id=1, source_target_pairs={{16,32},{48,64},{80,96},{112,128},{144,160},{176,192},{208,224},{2... | collective-permute-start | bytes 393224 | tf_op jit(solution)/shard_map/ppermute | solution.py:346
  13.6 3.6 %collective-permute-start.1 = (bf16[8,2,32,128]{3,2,1,0:T(8,128)(2,1)S(1)}, bf16[8,2,32,128]{3,2,1,0:T(8,128)(2,1)S(1)}, u32[]{:S(2)}, u32[]{:S(2)}) collective-permute-start(bf16[8,2,32,128]{3,2,1,0:T(8,128)(2,1)S(1)} %get-tuple-element.15.raw_ref), channel_id=1, source_target_pairs={{224,240},{240,224},{225,241},{241,225},{226,242},{242,226},{227,2... | collective-permute-start | bytes 393224 | tf_op jit(solution)/shard_map/ppermute | solution.py:346
  17.2 9.0 %collective-permute-start.3 = (bf16[6,32,128]{2,1,0:T(8,128)(2,1)S(1)}, bf16[6,32,128]{2,1,0:T(8,128)(2,1)S(1)}, u32[]{:S(2)}, u32[]{:S(2)}) collective-permute-start(bf16[6,32,128]{2,1,0:T(8,128)(2,1)S(1)} %get-tuple-element.20), channel_id=1, source_target_pairs={{1,2},{3,4},{5,6},{7,8},{9,10},{11,12},{13,14},{2,1},{4,3},{6,5},{... | collective-permute-start | bytes 147464 | tf_op jit(solution)/shard_map/ppermute | solution.py:346
  21.5 4.7 %collective-permute-start.4 = (bf16[6,32,128]{2,1,0:T(8,128)(2,1)S(1)}, bf16[6,32,128]{2,1,0:T(8,128)(2,1)S(1)}, u32[]{:S(2)}, u32[]{:S(2)}) collective-permute-start(bf16[6,32,128]{2,1,0:T(8,128)(2,1)S(1)} %get-tuple-element.21), channel_id=1, source_target_pairs={{0,1},{2,3},{4,5},{6,7},{8,9},{10,11},{12,13},{14,15},{1,0},{3,2},... | collective-permute-start | bytes 147464 | tf_op jit(solution)/shard_map/ppermute | solution.py:346

commit v5 on v4

--- a/solution.py
+++ b/solution.py
@@ -264,20 +264,24 @@
         mid_ref[k] = jnp.dot(mix_ref[...], smooth, preferred_element_type=F32)
 
 
-def side_block(raw_ref, side, bands_ref, mix_ref, ends_ref):
+def side_block(raw_ref, side, bands_ref, ends_ref):
     groups = raw_ref.shape[0] // 3
     left = jnp.concatenate([render(raw_ref[at]) for at in range(3 * groups)], axis=1)
     right = jnp.concatenate([bands_ref[t, 2 * side] for t in range(3)], axis=0)
     smooth = ends_ref[side] + jnp.dot(left, right, preferred_element_type=F32)
-    return jnp.dot(mix_ref[...], smooth.astype(BF16), preferred_element_type=F32)
+    return smooth.astype(BF16)
 
 
 def finish_kernel(
     outer_ref, inner_ref, bands_ref, mix_ref, ends_ref, mid_ref, out_hbm, out_ref, sems
 ):
     groups = outer_ref.shape[0] // 3
-    outer = side_block(outer_ref, parity(), bands_ref, mix_ref, ends_ref)
-    inner = side_block(inner_ref, 1 - parity(), bands_ref, mix_ref, ends_ref)
+    smooth = [
+        side_block(outer_ref, parity(), bands_ref, ends_ref),
+        side_block(inner_ref, 1 - parity(), bands_ref, ends_ref),
+    ]
+    both = jnp.dot(mix_ref[...], jnp.concatenate(smooth, axis=1), preferred_element_type=F32)
+    outer, inner = both[:, : 2 * LANES], both[:, 2 * LANES :]
     odd = parity() == 1
     mixed = [jnp.where(odd, inner, outer)]
     mixed += [mid_ref[k] for k in range(mid_ref.shape[0])]

time: 28 us -> 27.9 us (level)
  no operation moved by 1% of the time
where the time goes in v5:
time: 27.9 us; the launch traced here: 27.7 us
  starting transfers between devices  19.3 us (69%)
  Pallas kernels  6.53 us (23%)
  waiting for transfers between devices  1.77 us (6%)
    ppermute x5, starting transfers between devices, swapped(): return lax.ppermute(array, axis, pairs + [(j, i) for i, j in pairs])  19.3 us
    pallas_call x6, Pallas kernels, call(): pl.pallas_call(kernel, out_shape=out, in_specs=[whole] * len(args) + [pl....  6.53 us
    ppermute x5, waiting for transfers between devices, swapped(): return lax.ppermute(array, axis, pairs + [(j, i) for i, j in pairs])  1.77 us
  transfers between devices with their start and end apart: 5, of which 2 were waited for; matrix products, arithmetic and copies ran while one was open for 0% of the time, Pallas kernels for 14%

profile of v5, /device:TPU:6, one launch (start us, length us, event | category | flops | bytes accessed | tf_op | source)
XLA Modules:
  0.0 27.7 jit_solution(13944741124133337620)
XLA Ops:
  0.0 1.2 %shard_map.55 = (bf16[8,2,32,128]{3,2,1,0:T(8,128)(2,1)S(1)}, bf16[33,33]{1,0:T(8,128)(2,1)S(1)}, bf16[30,64]{1,0:T(8,128)(2,1)S(1)}) custom-call(s32[2,7,16,128]{3,2,1,0:T(8,128)} %bounds_hbm.1, s32[2,16,128]{2,1,0:T(8,128)} %count_hbm.1, bf16[2,8,16,128]{3,2,1,0:T(8,128)(2,1)} %values_hbm.1, bf16[33,33]{1,0:T(8,128)(2,1)} %footprint_hbm.1, ...), custom_call_target="tpu_custom_call" | custom-call | tf_op jit(solution)/shard_map/pallas_call | solution.py:327
  1.2 3.8 %collective-permute-start.2 = (bf16[8,2,32,128]{3,2,1,0:T(8,128)(2,1)S(1)}, bf16[8,2,32,128]{3,2,1,0:T(8,128)(2,1)S(1)}, u32[]{:S(2)}, u32[]{:S(2)}) collective-permute-start(bf16[8,2,32,128]{3,2,1,0:T(8,128)(2,1)S(1)} %get-tuple-element.15.raw_ref), channel_id=1, source_target_pairs={{0,16},{32,48},{64,80},{96,112},{128,144},{160,176},{192,208},{256... | collective-permute-start | bytes 393224 | tf_op jit(solution)/shard_map/ppermute | solution.py:350
  5.0 8.5 %collective-permute-start = (bf16[8,2,32,128]{3,2,1,0:T(8,128)(2,1)S(1)}, bf16[8,2,32,128]{3,2,1,0:T(8,128)(2,1)S(1)}, u32[]{:S(2)}, u32[]{:S(2)}) collective-permute-start(bf16[8,2,32,128]{3,2,1,0:T(8,128)(2,1)S(1)} %get-tuple-element.15.raw_ref), channel_id=1, source_target_pairs={{16,32},{48,64},{80,96},{112,128},{144,160},{176,192},{208,224},{2... | collective-permute-start | bytes 393224 | tf_op jit(solution)/shard_map/ppermute | solution.py:350
  13.6 0.7 %collective-permute-start.1 = (bf16[8,2,32,128]{3,2,1,0:T(8,128)(2,1)S(1)}, bf16[8,2,32,128]{3,2,1,0:T(8,128)(2,1)S(1)}, u32[]{:S(2)}, u32[]{:S(2)}) collective-permute-start(bf16[8,2,32,128]{3,2,1,0:T(8,128)(2,1)S(1)} %get-tuple-element.15.raw_ref), channel_id=1, source_target_pairs={{224,240},{240,224},{225,241},{241,225},{226,242},{242,226},{227,2... | collective-permute-start | bytes 393224 | tf_op jit(solution)/shard_map/ppermute | solution.py:350
  14.2 1.5 %shard_map.56 = (f32[1024,256]{1,0:T(8,128)S(1)}, bf16[3,3,256,256]{3,2,1,0:T(8,128)(2,1)S(1)}, bf16[64,128]{1,0:T(8,128)(2,1)S(1)}) custom-call(bf16[8,2,32,128]{3,2,1,0:T(8,128)(2,1)S(1)} %get-tuple-element.15.raw_ref, bf16[33,33]{1,0:T(8,128)(2,1)S(1)} %get-tuple-element.16.footprint_ref, bf16[30,64]{1,0:T(8,128)(2,1)S(1)} %get-tuple-element.17.gates_ref), custom_call_target="tpu_custom_call" | custom-call | flops 2000000000 | tf_op jit(solution)/shard_map/pallas_call | solution.py:327
  15.7 0.0 collective-permute-done.2.raw_ref.first_ref
  15.7 1.1 %shard_map.57.total_ref = f32[1024,256]{1,0:T(8,128)S(1)} custom-call(bf16[8,2,32,128]{3,2,1,0:T(8,128)(2,1)S(1)} %collective-permute-done.2.raw_ref.first_ref, bf16[3,3,256,256]{3,2,1,0:T(8,128)(2,1)S(1)} %get-tuple-element.18.bands_ref, f32[1024,256]{1,0:T(8,128)S(1)} %get-tuple-element.19.total_ref), custom_call_target="tpu_custom_call", output_to_operand_aliasing={{}: (2, {})} | custom-call | flops 1000000000 | tf_op jit(solution)/shard_map/pallas_call | solution.py:327
  16.8 0.3 %collective-permute-done.second_ref = bf16[8,2,32,128]{3,2,1,0:T(8,128)(2,1)S(1)} collective-permute-done((bf16[8,2,32,128]{3,2,1,0:T(8,128)(2,1)S(1)}, bf16[8,2,32,128]{3,2,1,0:T(8,128)(2,1)S(1)}, u32[]{:S(2)}, u32[]{:S(2)}) %collective-permute-start) | collective-permute-done | bytes 131104 | tf_op jit(solution)/shard_map/ppermute | solution.py:350
  17.1 0.0 collective-permute-done.1.late_ref
  17.2 4.4 %collective-permute-start.3 = (bf16[6,32,128]{2,1,0:T(8,128)(2,1)S(1)}, bf16[6,32,128]{2,1,0:T(8,128)(2,1)S(1)}, u32[]{:S(2)}, u32[]{:S(2)}) collective-permute-start(bf16[6,32,128]{2,1,0:T(8,128)(2,1)S(1)} %get-tuple-element.20), channel_id=1, source_target_pairs={{1,2},{3,4},{5,6},{7,8},{9,10},{11,12},{13,14},{2,1},{4,3},{6,5},{... | collective-permute-start | bytes 147464 | tf_op jit(solution)/shard_map/ppermute | solution.py:350
  21.5 1.9 %collective-permute-start.4 = (bf16[6,32,128]{2,1,0:T(8,128)(2,1)S(1)}, bf16[6,32,128]{2,1,0:T(8,128)(2,1)S(1)}, u32[]{:S(2)}, u32[]{:S(2)}) collective-permute-start(bf16[6,32,128]{2,1,0:T(8,128)(2,1)S(1)} %get-tuple-element.21), channel_id=1, source_target_pairs={{0,1},{2,3},{4,5},{6,7},{8,9},{10,11},{12,13},{14,15},{1,0},{3,2},... | collective-permute-start | bytes 147464 | tf_op jit(solution)/shard_map/ppermute | solution.py:350
  23.5 1.3 %shard_map.59 = (f32[2,128,256]{2,1,0:T(8,128)S(1)}, f32[6,64,256]{2,1,0:T(8,128)S(1)}) custom-call(bf16[8,2,32,128]{3,2,1,0:T(8,128)(2,1)S(1)} %collective-permute-done.second_ref, bf16[8,2,32,128]{3,2,1,0:T(8,128)(2,1)S(1)} %collective-permute-done.1.late_ref, bf16[3,3,256,256]{3,2,1,0:T(8,128)(2,1)S(1)} %get-tuple-element.18.bands_ref, ...), custom_call_target="tpu_custom_call" | custom-call | flops 1000000000 | tf_op jit(solution)/shard_map/pallas_call | solution.py:327
  24.7 1.5 %collective-permute-done.3.outer_ref = bf16[6,32,128]{2,1,0:T(8,128)(2,1)S(1)} collective-permute-done((bf16[6,32,128]{2,1,0:T(8,128)(2,1)S(1)}, bf16[6,32,128]{2,1,0:T(8,128)(2,1)S(1)}, u32[]{:S(2)}, u32[]{:S(2)}) %collective-permute-start.3) | collective-permute-done | bytes 49184 | tf_op jit(solution)/shard_map/ppermute | solution.py:350
  26.2 0.0 collective-permute-done.4.inner_ref
  26.2 1.5 %shard_map.60 = f32[960,128]{1,0:T(8,128)} custom-call(bf16[6,32,128]{2,1,0:T(8,128)(2,1)S(1)} %collective-permute-done.3.outer_ref, bf16[6,32,128]{2,1,0:T(8,128)(2,1)S(1)} %collective-permute-done.4.inner_ref, bf16[3,3,256,256]{3,2,1,0:T(8,128)(2,1)S(1)} %get-tuple-element.18.bands_ref, bf16[64,128]{1,0:T(8,128)(2,1)S(1)} %get-tuple-element.22.mix_ref, ...), custom_call_target="tpu_custom_call" | custom-call | tf_op jit(solution)/shard_map/pallas_call | solution.py:327
  (1 shorter events, 0.0 us)
Async XLA Ops:
  1.2 14.5 %collective-permute-start.2 = (bf16[8,2,32,128]{3,2,1,0:T(8,128)(2,1)S(1)}, bf16[8,2,32,128]{3,2,1,0:T(8,128)(2,1)S(1)}, u32[]{:S(2)}, u32[]{:S(2)}) collective-permute-start(bf16[8,2,32,128]{3,2,1,0:T(8,128)(2,1)S(1)} %get-tuple-element.15.raw_ref), channel_id=1, source_target_pairs={{0,16},{32,48},{64,80},{96,112},{128,144},{160,176},{192,208},{256... | collective-permute-start | bytes 393224 | tf_op jit(solution)/shard_map/ppermute | solution.py:350
  5.0 12.1 %collective-permute-start = (bf16[8,2,32,128]{3,2,1,0:T(8,128)(2,1)S(1)}, bf16[8,2,32,128]{3,2,1,0:T(8,128)(2,1)S(1)}, u32[]{:S(2)}, u32[]{:S(2)}) collective-permute-start(bf16[8,2,32,128]{3,2,1,0:T(8,128)(2,1)S(1)} %get-tuple-element.15.raw_ref), channel_id=1, source_target_pairs={{16,32},{48,64},{80,96},{112,128},{144,160},{176,192},{208,224},{2... | collective-permute-start | bytes 393224 | tf_op jit(solution)/shard_map/ppermute | solution.py:350
  13.6 3.6 %collective-permute-start.1 = (bf16[8,2,32,128]{3,2,1,0:T(8,128)(2,1)S(1)}, bf16[8,2,32,128]{3,2,1,0:T(8,128)(2,1)S(1)}, u32[]{:S(2)}, u32[]{:S(2)}) collective-permute-start(bf16[8,2,32,128]{3,2,1,0:T(8,128)(2,1)S(1)} %get-tuple-element.15.raw_ref), channel_id=1, source_target_pairs={{224,240},{240,224},{225,241},{241,225},{226,242},{242,226},{227,2... | collective-permute-start | bytes 393224 | tf_op jit(solution)/shard_map/ppermute | solution.py:350
  17.2 9.0 %collective-permute-start.3 = (bf16[6,32,128]{2,1,0:T(8,128)(2,1)S(1)}, bf16[6,32,128]{2,1,0:T(8,128)(2,1)S(1)}, u32[]{:S(2)}, u32[]{:S(2)}) collective-permute-start(bf16[6,32,128]{2,1,0:T(8,128)(2,1)S(1)} %get-tuple-element.20), channel_id=1, source_target_pairs={{1,2},{3,4},{5,6},{7,8},{9,10},{11,12},{13,14},{2,1},{4,3},{6,5},{... | collective-permute-start | bytes 147464 | tf_op jit(solution)/shard_map/ppermute | solution.py:350
  21.5 4.7 %collective-permute-start.4 = (bf16[6,32,128]{2,1,0:T(8,128)(2,1)S(1)}, bf16[6,32,128]{2,1,0:T(8,128)(2,1)S(1)}, u32[]{:S(2)}, u32[]{:S(2)}) collective-permute-start(bf16[6,32,128]{2,1,0:T(8,128)(2,1)S(1)} %get-tuple-element.21), channel_id=1, source_target_pairs={{0,1},{2,3},{4,5},{6,7},{8,9},{10,11},{12,13},{14,15},{1,0},{3,2},... | collective-permute-start | bytes 147464 | tf_op jit(solution)/shard_map/ppermute | solution.py:350

commit v6 on v5

--- a/solution.py
+++ b/solution.py
@@ -276,16 +276,16 @@
     outer_ref, inner_ref, bands_ref, mix_ref, ends_ref, mid_ref, out_hbm, out_ref, sems
 ):
     groups = outer_ref.shape[0] // 3
+    odd = parity() == 1
+    outer, inner = outer_ref[...], inner_ref[...]
     smooth = [
-        side_block(outer_ref, parity(), bands_ref, ends_ref),
-        side_block(inner_ref, 1 - parity(), bands_ref, ends_ref),
+        side_block(jnp.where(odd, inner, outer), 0, bands_ref, ends_ref),
+        side_block(jnp.where(odd, outer, inner), 1, bands_ref, ends_ref),
     ]
     both = jnp.dot(mix_ref[...], jnp.concatenate(smooth, axis=1), preferred_element_type=F32)
-    outer, inner = both[:, : 2 * LANES], both[:, 2 * LANES :]
-    odd = parity() == 1
-    mixed = [jnp.where(odd, inner, outer)]
+    mixed = [both[:, : 2 * LANES]]
     mixed += [mid_ref[k] for k in range(mid_ref.shape[0])]
-    mixed += [jnp.where(odd, outer, inner)]
+    mixed += [both[:, 2 * LANES :]]
     half = mix_ref.shape[0] // 2
     rows = groups * ROWS
     gates = out_ref.shape[0] // (2 * rows)

time: 27.9 us -> 27.9 us (level)
  no operation moved by 1% of the time
where the time goes in v6:
time: 27.9 us; the launch traced here: 27.7 us
  starting transfers between devices  19.3 us (69%)
  Pallas kernels  6.56 us (24%)
  waiting for transfers between devices  1.77 us (6%)
    ppermute x5, starting transfers between devices, swapped(): return lax.ppermute(array, axis, pairs + [(j, i) for i, j in pairs])  19.3 us
    pallas_call x6, Pallas kernels, call(): pl.pallas_call(kernel, out_shape=out, in_specs=[whole] * len(args) + [pl....  6.56 us
    ppermute x5, waiting for transfers between devices, swapped(): return lax.ppermute(array, axis, pairs + [(j, i) for i, j in pairs])  1.77 us
  transfers between devices with their start and end apart: 5, of which 2 were waited for; matrix products, arithmetic and copies ran while one was open for 0% of the time, Pallas kernels for 14%

profile of v6, /device:TPU:6, one launch (start us, length us, event | category | flops | bytes accessed | tf_op | source)
XLA Modules:
  0.0 27.7 jit_solution(272733374826579688)
XLA Ops:
  0.0 1.2 %shard_map.55 = (bf16[8,2,32,128]{3,2,1,0:T(8,128)(2,1)S(1)}, bf16[33,33]{1,0:T(8,128)(2,1)S(1)}, bf16[30,64]{1,0:T(8,128)(2,1)S(1)}) custom-call(s32[2,7,16,128]{3,2,1,0:T(8,128)} %bounds_hbm.1, s32[2,16,128]{2,1,0:T(8,128)} %count_hbm.1, bf16[2,8,16,128]{3,2,1,0:T(8,128)(2,1)} %values_hbm.1, bf16[33,33]{1,0:T(8,128)(2,1)} %footprint_hbm.1, ...), custom_call_target="tpu_custom_call" | custom-call | tf_op jit(solution)/shard_map/pallas_call | solution.py:327
  1.2 3.8 %collective-permute-start.2 = (bf16[8,2,32,128]{3,2,1,0:T(8,128)(2,1)S(1)}, bf16[8,2,32,128]{3,2,1,0:T(8,128)(2,1)S(1)}, u32[]{:S(2)}, u32[]{:S(2)}) collective-permute-start(bf16[8,2,32,128]{3,2,1,0:T(8,128)(2,1)S(1)} %get-tuple-element.15.raw_ref), channel_id=1, source_target_pairs={{0,16},{32,48},{64,80},{96,112},{128,144},{160,176},{192,208},{256... | collective-permute-start | bytes 393224 | tf_op jit(solution)/shard_map/ppermute | solution.py:350
  5.0 8.5 %collective-permute-start = (bf16[8,2,32,128]{3,2,1,0:T(8,128)(2,1)S(1)}, bf16[8,2,32,128]{3,2,1,0:T(8,128)(2,1)S(1)}, u32[]{:S(2)}, u32[]{:S(2)}) collective-permute-start(bf16[8,2,32,128]{3,2,1,0:T(8,128)(2,1)S(1)} %get-tuple-element.15.raw_ref), channel_id=1, source_target_pairs={{16,32},{48,64},{80,96},{112,128},{144,160},{176,192},{208,224},{2... | collective-permute-start | bytes 393224 | tf_op jit(solution)/shard_map/ppermute | solution.py:350
  13.6 0.7 %collective-permute-start.1 = (bf16[8,2,32,128]{3,2,1,0:T(8,128)(2,1)S(1)}, bf16[8,2,32,128]{3,2,1,0:T(8,128)(2,1)S(1)}, u32[]{:S(2)}, u32[]{:S(2)}) collective-permute-start(bf16[8,2,32,128]{3,2,1,0:T(8,128)(2,1)S(1)} %get-tuple-element.15.raw_ref), channel_id=1, source_target_pairs={{224,240},{240,224},{225,241},{241,225},{226,242},{242,226},{227,2... | collective-permute-start | bytes 393224 | tf_op jit(solution)/shard_map/ppermute | solution.py:350
  14.2 1.5 %shard_map.56 = (f32[1024,256]{1,0:T(8,128)S(1)}, bf16[3,3,256,256]{3,2,1,0:T(8,128)(2,1)S(1)}, bf16[64,128]{1,0:T(8,128)(2,1)S(1)}) custom-call(bf16[8,2,32,128]{3,2,1,0:T(8,128)(2,1)S(1)} %get-tuple-element.15.raw_ref, bf16[33,33]{1,0:T(8,128)(2,1)S(1)} %get-tuple-element.16.footprint_ref, bf16[30,64]{1,0:T(8,128)(2,1)S(1)} %get-tuple-element.17.gates_ref), custom_call_target="tpu_custom_call" | custom-call | flops 2000000000 | tf_op jit(solution)/shard_map/pallas_call | solution.py:327
  15.7 0.0 collective-permute-done.2.raw_ref.first_ref
  15.7 1.1 %shard_map.57.total_ref = f32[1024,256]{1,0:T(8,128)S(1)} custom-call(bf16[8,2,32,128]{3,2,1,0:T(8,128)(2,1)S(1)} %collective-permute-done.2.raw_ref.first_ref, bf16[3,3,256,256]{3,2,1,0:T(8,128)(2,1)S(1)} %get-tuple-element.18.bands_ref, f32[1024,256]{1,0:T(8,128)S(1)} %get-tuple-element.19.total_ref), custom_call_target="tpu_custom_call", output_to_operand_aliasing={{}: (2, {})} | custom-call | flops 1000000000 | tf_op jit(solution)/shard_map/pallas_call | solution.py:327
  16.8 0.3 %collective-permute-done.second_ref = bf16[8,2,32,128]{3,2,1,0:T(8,128)(2,1)S(1)} collective-permute-done((bf16[8,2,32,128]{3,2,1,0:T(8,128)(2,1)S(1)}, bf16[8,2,32,128]{3,2,1,0:T(8,128)(2,1)S(1)}, u32[]{:S(2)}, u32[]{:S(2)}) %collective-permute-start) | collective-permute-done | bytes 131104 | tf_op jit(solution)/shard_map/ppermute | solution.py:350
  17.1 0.0 collective-permute-done.1.late_ref
  17.2 4.4 %collective-permute-start.3 = (bf16[6,32,128]{2,1,0:T(8,128)(2,1)S(1)}, bf16[6,32,128]{2,1,0:T(8,128)(2,1)S(1)}, u32[]{:S(2)}, u32[]{:S(2)}) collective-permute-start(bf16[6,32,128]{2,1,0:T(8,128)(2,1)S(1)} %get-tuple-element.20), channel_id=1, source_target_pairs={{1,2},{3,4},{5,6},{7,8},{9,10},{11,12},{13,14},{2,1},{4,3},{6,5},{... | collective-permute-start | bytes 147464 | tf_op jit(solution)/shard_map/ppermute | solution.py:350
  21.5 1.9 %collective-permute-start.4 = (bf16[6,32,128]{2,1,0:T(8,128)(2,1)S(1)}, bf16[6,32,128]{2,1,0:T(8,128)(2,1)S(1)}, u32[]{:S(2)}, u32[]{:S(2)}) collective-permute-start(bf16[6,32,128]{2,1,0:T(8,128)(2,1)S(1)} %get-tuple-element.21), channel_id=1, source_target_pairs={{0,1},{2,3},{4,5},{6,7},{8,9},{10,11},{12,13},{14,15},{1,0},{3,2},... | collective-permute-start | bytes 147464 | tf_op jit(solution)/shard_map/ppermute | solution.py:350
  23.5 1.3 %shard_map.59 = (f32[2,128,256]{2,1,0:T(8,128)S(1)}, f32[6,64,256]{2,1,0:T(8,128)S(1)}) custom-call(bf16[8,2,32,128]{3,2,1,0:T(8,128)(2,1)S(1)} %collective-permute-done.second_ref, bf16[8,2,32,128]{3,2,1,0:T(8,128)(2,1)S(1)} %collective-permute-done.1.late_ref, bf16[3,3,256,256]{3,2,1,0:T(8,128)(2,1)S(1)} %get-tuple-element.18.bands_ref, ...), custom_call_target="tpu_custom_call" | custom-call | flops 1000000000 | tf_op jit(solution)/shard_map/pallas_call | solution.py:327
  24.7 1.5 %collective-permute-done.3.outer_ref = bf16[6,32,128]{2,1,0:T(8,128)(2,1)S(1)} collective-permute-done((bf16[6,32,128]{2,1,0:T(8,128)(2,1)S(1)}, bf16[6,32,128]{2,1,0:T(8,128)(2,1)S(1)}, u32[]{:S(2)}, u32[]{:S(2)}) %collective-permute-start.3) | collective-permute-done | bytes 49184 | tf_op jit(solution)/shard_map/ppermute | solution.py:350
  26.2 0.0 collective-permute-done.4.inner_ref
  26.2 1.5 %shard_map.60 = f32[960,128]{1,0:T(8,128)} custom-call(bf16[6,32,128]{2,1,0:T(8,128)(2,1)S(1)} %collective-permute-done.3.outer_ref, bf16[6,32,128]{2,1,0:T(8,128)(2,1)S(1)} %collective-permute-done.4.inner_ref, bf16[3,3,256,256]{3,2,1,0:T(8,128)(2,1)S(1)} %get-tuple-element.18.bands_ref, bf16[64,128]{1,0:T(8,128)(2,1)S(1)} %get-tuple-element.22.mix_ref, ...), custom_call_target="tpu_custom_call" | custom-call | tf_op jit(solution)/shard_map/pallas_call | solution.py:327
  (1 shorter events, 0.0 us)
Async XLA Ops:
  1.2 14.5 %collective-permute-start.2 = (bf16[8,2,32,128]{3,2,1,0:T(8,128)(2,1)S(1)}, bf16[8,2,32,128]{3,2,1,0:T(8,128)(2,1)S(1)}, u32[]{:S(2)}, u32[]{:S(2)}) collective-permute-start(bf16[8,2,32,128]{3,2,1,0:T(8,128)(2,1)S(1)} %get-tuple-element.15.raw_ref), channel_id=1, source_target_pairs={{0,16},{32,48},{64,80},{96,112},{128,144},{160,176},{192,208},{256... | collective-permute-start | bytes 393224 | tf_op jit(solution)/shard_map/ppermute | solution.py:350
  5.0 12.1 %collective-permute-start = (bf16[8,2,32,128]{3,2,1,0:T(8,128)(2,1)S(1)}, bf16[8,2,32,128]{3,2,1,0:T(8,128)(2,1)S(1)}, u32[]{:S(2)}, u32[]{:S(2)}) collective-permute-start(bf16[8,2,32,128]{3,2,1,0:T(8,128)(2,1)S(1)} %get-tuple-element.15.raw_ref), channel_id=1, source_target_pairs={{16,32},{48,64},{80,96},{112,128},{144,160},{176,192},{208,224},{2... | collective-permute-start | bytes 393224 | tf_op jit(solution)/shard_map/ppermute | solution.py:350
  13.6 3.6 %collective-permute-start.1 = (bf16[8,2,32,128]{3,2,1,0:T(8,128)(2,1)S(1)}, bf16[8,2,32,128]{3,2,1,0:T(8,128)(2,1)S(1)}, u32[]{:S(2)}, u32[]{:S(2)}) collective-permute-start(bf16[8,2,32,128]{3,2,1,0:T(8,128)(2,1)S(1)} %get-tuple-element.15.raw_ref), channel_id=1, source_target_pairs={{224,240},{240,224},{225,241},{241,225},{226,242},{242,226},{227,2... | collective-permute-start | bytes 393224 | tf_op jit(solution)/shard_map/ppermute | solution.py:350
  17.2 9.0 %collective-permute-start.3 = (bf16[6,32,128]{2,1,0:T(8,128)(2,1)S(1)}, bf16[6,32,128]{2,1,0:T(8,128)(2,1)S(1)}, u32[]{:S(2)}, u32[]{:S(2)}) collective-permute-start(bf16[6,32,128]{2,1,0:T(8,128)(2,1)S(1)} %get-tuple-element.20), channel_id=1, source_target_pairs={{1,2},{3,4},{5,6},{7,8},{9,10},{11,12},{13,14},{2,1},{4,3},{6,5},{... | collective-permute-start | bytes 147464 | tf_op jit(solution)/shard_map/ppermute | solution.py:350
  21.5 4.7 %collective-permute-start.4 = (bf16[6,32,128]{2,1,0:T(8,128)(2,1)S(1)}, bf16[6,32,128]{2,1,0:T(8,128)(2,1)S(1)}, u32[]{:S(2)}, u32[]{:S(2)}) collective-permute-start(bf16[6,32,128]{2,1,0:T(8,128)(2,1)S(1)} %get-tuple-element.21), channel_id=1, source_target_pairs={{0,1},{2,3},{4,5},{6,7},{8,9},{10,11},{12,13},{14,15},{1,0},{3,2},... | collective-permute-start | bytes 147464 | tf_op jit(solution)/shard_map/ppermute | solution.py:350
